TPU v7x, 512 devices: a whole 4x4x16 slice. The times are simulated.
512 devices in a mesh: hull: 128 (over z, x, core), freq: 4 (over y).
Axes of the slice: x: 4, y: 4, z: 16, core: 2. Of those that a mesh axis runs over, the one named last changes fastest.
Arguments:
- wave_loads: bfloat16 [4, 128, 2, 36, 384], P('freq', 'hull'), may hold values from -0.47851562 to 0.47851562
- pivot_inverse: bfloat16 [4, 128, 2, 384, 384], P('freq', 'hull'), may hold values from -2.2 to 2.2
- forward_factor: bfloat16 [4, 128, 384], P('freq', 'hull'), may hold values from -1 to 1
- backward_factor: bfloat16 [4, 128, 384], P('freq', 'hull'), may hold values from -1 to 1
- recovery: bfloat16 [128, 256, 768], P('hull'), may hold values from -0.21875 to 0.21875
- hotspots: int32 [128, 256], P('hull'), may hold values from 0 to 255
- frequency: float32 [4], P('freq'), may hold values from 0.3 to 1.5
- spectrum: float32 [4, 36], P('freq'), may hold values from 0.1 to 7
Outputs:
- displacement: float32 [4, 128, 2, 36, 384], P('freq', 'hull')
- moments: float32 [3, 128, 36, 256], P(None, 'hull')
- log_damage: float32 [128, 36, 256], P('hull')
All inputs are finite; a program needn't handle non-finite values.
Results may differ from a plain program's by a relative error of at most 0.0003.
Values may be sent and summed in bfloat16 or wider, within the bound.
No kernel may reach another device: no remote copies, remote signals or barrier semaphores. Data moves between devices by JAX's collectives and lax.ppermute only.
A program may use at most 64 MiB of HBM per device.

v0:
```python
import jax
import jax.numpy as jnp
from jax import lax
from jax.sharding import PartitionSpec as P

precise = lax.Precision.HIGHEST


def carried_in(part, axis, combine, identity, reverse):
    count = lax.axis_size(axis)
    place = lax.axis_index(axis)
    ahead = count - 1 - place if reverse else place
    gathered = jax.tree.map(lambda a: lax.all_gather(a, axis), part)
    state = jax.tree.map(lambda a, e: jnp.zeros_like(a) + jnp.asarray(e, a.dtype), part, identity)

    def one(hop, state):
        source = count - 1 - hop if reverse else hop
        return combine(
            state, jax.tree.map(lambda a: lax.dynamic_index_in_dim(a, source, 0, False), gathered)
        )

    return lax.fori_loop(0, ahead, one, state)


def shifted(value, axis, steps):
    count = lax.axis_size(axis)
    initial, last = (max(0, -steps), min(count, count - steps))
    return lax.ppermute(value, axis, [(source, source + steps) for source in range(initial, last)])


def complex_lowp(left_side, right_side):
    real_left = left_side[..., 0, :, :]
    imag_left = left_side[..., 1, :, :]
    real_right = right_side[..., 0, :, :]
    imag_right = right_side[..., 1, :, :]
    real_part = jnp.matmul(real_left, real_right, preferred_element_type=jnp.float32) - jnp.matmul(
        imag_left, imag_right, preferred_element_type=jnp.float32
    )
    imag_part = jnp.matmul(real_left, imag_right, preferred_element_type=jnp.float32) + jnp.matmul(
        imag_left, real_right, preferred_element_type=jnp.float32
    )
    return jnp.stack([real_part, imag_part], axis=-3)


def apply_modal(vectors, factors):
    return vectors * factors[:, None, None, :]


def compose(earlier, later):
    return (later[0] + apply_modal(earlier[0], later[1]), earlier[1] * later[1])


def identity_maps(front_shape, factor_shape):
    return (jnp.zeros(front_shape, jnp.float32), jnp.ones(factor_shape, jnp.float32))


def fatigue(moments):
    zeroth = moments[0]
    second = moments[1]
    fourth = moments[2]
    return (
        0.5 * jnp.log(fourth / second)
        + 1.5 * jnp.log(zeroth)
        + jnp.log(0.5 + 0.5 * second / jnp.sqrt(zeroth * fourth))
    )


def per_device(
    wave_loads,
    pivot_inverse,
    forward_factor,
    backward_factor,
    recovery,
    hotspots,
    frequency,
    spectrum,
):
    source = complex_lowp(wave_loads[:, 0], pivot_inverse[:, 0])
    forward_maps = -forward_factor[:, 0].astype(jnp.float32)
    backward_maps = -backward_factor[:, 0].astype(jnp.float32)
    identity = identity_maps(source.shape, forward_maps.shape)
    before = carried_in((source, forward_maps), "hull", compose, identity, False)[0]
    front_now = source + apply_modal(before, forward_maps)
    behind = carried_in((front_now, backward_maps), "hull", compose, identity, True)[0]
    motion = front_now + apply_modal(behind, backward_maps)
    stern = shifted(motion, "hull", 1)
    picked = jnp.take(recovery[0], hotspots[0], axis=0).astype(jnp.float32)
    half_width = picked.shape[1] // 2
    stress = jnp.matmul(stern, picked[:, :half_width].T, precision=precise) + jnp.matmul(
        motion, picked[:, half_width:].T, precision=precise
    )
    energy = stress[:, 0] ** 2 + stress[:, 1] ** 2
    spacing = 1.2 / (frequency.shape[0] * lax.axis_size("freq"))
    weighted = (spectrum * spacing)[:, :, None] * energy
    partial_sum = jnp.stack(
        [jnp.sum(weighted * (frequency**exponent)[:, None, None], axis=0) for exponent in (0, 2, 4)]
    )
    totals = lax.psum(partial_sum, "freq")
    damage = fatigue(totals)
    return (motion[:, None], totals[:, None], damage[None])


def solution(mesh):
    in_specs = (
        P("freq", "hull", None, None, None),
        P("freq", "hull", None, None, None),
        P("freq", "hull", None),
        P("freq", "hull", None),
        P("hull", None, None),
        P("hull", None),
        P("freq"),
        P("freq", None),
    )
    out_specs = (
        P("freq", "hull", None, None, None),
        P(None, "hull", None, None),
        P("hull", None, None),
    )
    return jax.shard_map(
        per_device, mesh=mesh, in_specs=in_specs, out_specs=out_specs, check_vma=False
    )
```

profile of v0, /device:TPU:1, one launch (start us, length us, event | category | flops | bytes accessed | tf_op | source)
XLA Modules:
  0.0 640.5 jit_solution(11092787891500207744)
XLA Ops:
  8.1 1.1 fusion.6
  9.2 1.1 fusion.5
  10.4 1.1 fusion.3
  11.5 1.1 fusion.4
  14.2 103.1 %all_gather.22 = f32[128,1,384]{2,1,0:T(1,128)S(1)} all-gather(f32[1,1,384]{2,1,0:T(1,128)S(1)} %get-tuple-element.197), channel_id=1, replica_groups=mesh['hull'=128,'freq'=4] {'hull'}, dimensions={0}, use_global_device_ids=true | all-gather | bytes 198144 | tf_op jit(solution)/shard_map/all_gather | solution.py:13
  117.3 57.0 %all-gather.5.cloned.1.call-done = f32[128,2,36,384]{3,1,2,0:T(2,128)} async-done(((f32[1,2,36,384]{3,1,2,0:T(2,128)}), f32[128,2,36,384]{3,1,2,0:T(2,128)}) %all-gather.5.cloned.1.call-update) | async-done | bytes 14155792 | tf_op jit(solution)/shard_map/all_gather | solution.py:13
  174.3 1.0 while.26
  174.4 0.9 constant_dynamic-slice_fusion.4
  177.5 1.2 gather_fusion
  178.7 219.6 %all_gather.25 = f32[128,1,384]{2,1,0:T(1,128)S(1)} all-gather(f32[1,1,384]{2,1,0:T(1,128)S(1)} %get-tuple-element.198), channel_id=1, replica_groups=mesh['hull'=128,'freq'=4] {'hull'}, dimensions={0}, use_global_device_ids=true | all-gather | bytes 198144 | tf_op jit(solution)/shard_map/all_gather | solution.py:13
  399.8 51.7 %all-gather.7.cloned.1.call-done = f32[128,2,36,384]{3,1,2,0:T(2,128)} async-done(((f32[1,2,36,384]{3,1,2,0:T(2,128)}), f32[128,2,36,384]{3,1,2,0:T(2,128)}) %all-gather.7.cloned.1.call-update) | async-done | bytes 14155792 | tf_op jit(solution)/shard_map/all_gather | solution.py:13
  451.5 129.5 %while.27 = (s32[]{:T(128)}, f32[1,2,36,384]{3,2,1,0:T(8,128)S(1)}, s32[]{:T(128)}, f32[128,1,2,36,384]{4,2,3,0,1:T(2,128)}, f32[128,1,384]{2,1,0:T(1,128)S(1)},...) while((s32[]{:T(128)}, f32[1,2,36,384]{3,2,1,0:T(8,128)S(1)}, s32[]{:T(128)}, ...), condition=%wide.region_3.4_spmd, body=%wide.region_2.3_spmd.sunk | while | flops 55302 | bytes 557715 | solution.py:22
  452.5 0.9 constant_dynamic-slice_fusion.5
  455.6 0.9 constant_dynamic-slice_fusion.5
  456.6 0.9 constant_dynamic-slice_fusion.5
  459.7 0.9 constant_dynamic-slice_fusion.5
  460.8 0.9 constant_dynamic-slice_fusion.5
  463.8 0.9 constant_dynamic-slice_fusion.5
  464.9 0.9 constant_dynamic-slice_fusion.5
  468.0 0.9 constant_dynamic-slice_fusion.5
  472.1 0.9 constant_dynamic-slice_fusion.5
  475.1 0.9 constant_dynamic-slice_fusion.5
  476.2 0.9 constant_dynamic-slice_fusion.5
  479.3 0.9 constant_dynamic-slice_fusion.5
  480.3 0.9 constant_dynamic-slice_fusion.5
  483.4 0.9 constant_dynamic-slice_fusion.5
  484.4 0.9 constant_dynamic-slice_fusion.5
  487.5 0.9 constant_dynamic-slice_fusion.5
  581.0 1.9 collective-permute-start
  583.3 1.5 collective-permute-done
  586.6 44.2 %all-reduce.2.cloned.1.call-done = f32[3,36,256]{2,1,0:T(8,128)} async-done(((f32[3,36,256]{2,1,0:T(8,128)}), f32[3,36,256]{2,1,0:T(8,128)}) %all-reduce.2.cloned.1.call-update) | async-done | bytes 110608 | tf_op jit(solution)/shard_map/psum | solution.py:98
  630.8 1.7 copy.28
  (394 shorter events, 119.9 us)
Async XLA Ops:
  7.2 170.4 %copy-start = (bf16[1,256,768]{2,1,0:T(8,128)(2,1)S(1)}, bf16[1,256,768]{2,1,0:T(8,128)(2,1)}, u32[]{:S(2)}) copy-start(bf16[1,256,768]{2,1,0:T(8,128)(2,1)} %param.16) | copy-start | bytes 1179652
  7.2 167.1 %all-gather.5.cloned.1.call-start = ((), (), s32[]{:S(2)}) async-start(), calls=%async_computation.1 | async-start | bytes 14266368 | tf_op jit(solution)/shard_map/all_gather | solution.py:13
  13.4 438.1 %all-gather.7.cloned.1.call-start = ((), (), s32[]{:S(2)}) async-start(), calls=%async_computation.2 | async-start | bytes 14266368 | tf_op jit(solution)/shard_map/all_gather | solution.py:13
  176.1 454.6 %all-reduce.2.cloned.1.call-start = ((), (), s32[]{:S(2)}) async-start(), calls=%async_computation | async-start | bytes 245760 | tf_op jit(solution)/shard_map/psum | solution.py:98
  581.0 3.8 collective-permute-start
Sparse Core Ops, SparseCore 0:
  13.5 160.7 all-gather.4
  177.9 273.4 all-gather.6
  586.0 44.7 all-reduce.1
where the time goes:
time: 645 us; the launch traced here: 640 us
  blocking collectives  323 us (50%)
  waiting for transfers between devices  154 us (24%)
  local copies, waits for them, and re-layouts  128 us (20%)
  between operations  14.5 us (2%)
  other arithmetic  10.1 us (2%)
    all_gather x2, blocking collectives, carried_in(): gathered = jax.tree.map(lambda a: lax.all_gather(a, axis), part)  323 us
    dynamic_slice x254, local copies, waits for them, and re-layouts, one(): lax.dynamic_index_in_dim(a, source, 0, False)  121 us
    all_gather x2, waiting for transfers between devices, carried_in(): gathered = jax.tree.map(lambda a: lax.all_gather(a, axis), part)  109 us
    psum x1, waiting for transfers between devices, per_device(): totals = lax.psum(partial_sum, 'freq')  44.2 us
  transfers between devices with their start and end apart: 4, of which 4 were waited for; matrix products, arithmetic and copies ran while one was open for 1% of the time, Pallas kernels for 0%

commit v1 on v0

v1 whole, which is shorter than its diff:
```python
import jax
import jax.numpy as jnp
from jax import lax
from jax.experimental import pallas as pl
from jax.experimental.pallas import tpu as pltpu
from jax.sharding import Mesh, PartitionSpec as P

SPAN, PAIR, ACROSS, CORES = 8, 2, 4, 2
GROUP = PAIR * ACROSS * CORES
HEAD, MODES, POINTS = 36, 384, 256
HALF = 40
ROWS = 2 * HALF
SHARE = ROWS // GROUP
LANES = 128
TILES = MODES // LANES
INNER = ("zl", "x", "core")
F32 = jnp.float32
BF16 = jnp.bfloat16


def call(body, shapes, *args, vmem_mib=12, scratch=()):
    outs = [jax.ShapeDtypeStruct(shape, F32) for shape in shapes]
    return pl.pallas_call(
        body,
        out_shape=outs,
        in_specs=[pl.BlockSpec(memory_space=pltpu.VMEM)] * len(args),
        out_specs=[pl.BlockSpec(memory_space=pltpu.VMEM)] * len(outs),
        scratch_shapes=list(scratch),
        compiler_params=pltpu.CompilerParams(vmem_limit_bytes=vmem_mib * 2**20),
    )(*args)


def padded(rows):
    return jnp.concatenate([rows, jnp.zeros((HALF - HEAD, rows.shape[1]), rows.dtype)], axis=0)


def source_body(loads, pivot, forward, backward, out):
    real = padded(loads[0, 0, 0].astype(F32))
    imag = padded(loads[0, 0, 1].astype(F32))
    by_real = jnp.concatenate([real, imag], axis=0).astype(BF16)
    by_imag = jnp.concatenate([-imag, real], axis=0).astype(BF16)
    source = jnp.dot(by_real, pivot[0, 0, 0], preferred_element_type=F32) + jnp.dot(
        by_imag, pivot[0, 0, 1], preferred_element_type=F32
    )
    fore = -forward[...].astype(F32)
    back = -backward[...].astype(F32)
    blank = jnp.zeros((1, MODES), F32)
    for d in range(GROUP):
        out[d] = jnp.concatenate([source[SHARE * d : SHARE * (d + 1)], fore, back, blank], axis=0)


def reduce_body(got, out):
    front = got[0, 0:SHARE]
    gain = got[0, SHARE : SHARE + 1]
    fronts, gains = [front], [gain]
    for j in range(1, GROUP):
        fore = got[j, SHARE : SHARE + 1]
        front = got[j, 0:SHARE] + front * fore
        gain = gain * fore
        fronts.append(front)
        gains.append(gain)
    last_back = got[GROUP - 1, SHARE + 1 : SHARE + 2]
    motion, through, back_gain = front, gain, last_back
    for j in range(GROUP - 2, -1, -1):
        back = got[j, SHARE + 1 : SHARE + 2]
        motion = fronts[j] + motion * back
        through = gains[j] + through * back
        back_gain = back_gain * back
    blank = jnp.zeros((16 - 2 * SHARE - 4, MODES), F32)
    packed = jnp.concatenate([front, motion, gain, through, back_gain, last_back, blank], axis=0)
    for g in range(SPAN):
        out[g] = packed


def solve_body(place, got, ends, out, into, beyond, before):
    mine = place[0, 0]
    zero = jnp.zeros((SHARE, MODES), F32)
    into[0, 0:SHARE] = zero
    before[0, 0:1] = jnp.zeros((1, MODES), F32)
    arriving = [zero]
    for g in range(SPAN - 1):
        arriving.append(ends[g, 0:SHARE] + arriving[g] * ends[g, 2 * SHARE : 2 * SHARE + 1])
        into[g + 1, 0:SHARE] = arriving[g + 1]
        before[g + 1, 0:1] = ends[g, 2 * SHARE + 3 : 2 * SHARE + 4]
    returning = zero
    beyond[SPAN - 1, 0:SHARE] = zero
    for g in range(SPAN - 1, 0, -1):
        returning = (
            ends[g, SHARE : 2 * SHARE]
            + arriving[g] * ends[g, 2 * SHARE + 1 : 2 * SHARE + 2]
            + returning * ends[g, 2 * SHARE + 2 : 2 * SHARE + 3]
        )
        beyond[g - 1, 0:SHARE] = returning
    enter = into[mine, 0:SHARE]
    front = enter
    fronts = []
    for j in range(GROUP):
        front = got[j, 0:SHARE] + front * got[j, SHARE : SHARE + 1]
        fronts.append(front)
    motion = beyond[mine, 0:SHARE]
    motions = [None] * GROUP
    for j in range(GROUP - 1, -1, -1):
        motion = fronts[j] + motion * got[j, SHARE + 1 : SHARE + 2]
        motions[j] = motion
    previous = enter + motion * before[mine, 0:1]
    for j in range(GROUP):
        both = jnp.concatenate([motions[j], previous], axis=0)
        for t in range(TILES):
            out[j, 2 * SHARE * t : 2 * SHARE * (t + 1)] = both[:, LANES * t : LANES * (t + 1)]
        out[j, 2 * SHARE * TILES : 32] = jnp.zeros((32 - 2 * SHARE * TILES, LANES), F32)
        previous = motions[j]


def split(values, parts):
    pieces = []
    for _ in range(parts):
        piece = values.astype(BF16)
        values = values - piece.astype(F32)
        pieces.append(piece)
    return jnp.concatenate(pieces, axis=0)


def stress_body(got, recovery, hotspots, frequency, spectrum, motion_out, out, motion, stern):
    for d in range(GROUP):
        for t in range(TILES):
            lanes = slice(LANES * t, LANES * (t + 1))
            rows = slice(SHARE * d, SHARE * (d + 1))
            motion[rows, lanes] = got[d, 2 * SHARE * t : 2 * SHARE * t + SHARE]
            stern[rows, lanes] = got[d, 2 * SHARE * t + SHARE : 2 * SHARE * (t + 1)]
    motion_out[0, 0, 0] = motion[0:HEAD]
    motion_out[0, 0, 1] = motion[HALF : HALF + HEAD]
    contract = (((1,), (1,)), ((), ()))
    both = lax.dot_general(
        split(stern[...], 2), recovery[0, :, 0:MODES], contract, preferred_element_type=F32
    ) + lax.dot_general(
        split(motion[...], 2), recovery[0, :, MODES:], contract, preferred_element_type=F32
    )
    stress = both[0:ROWS] + both[ROWS:]
    power = stress[0:HALF] ** 2 + stress[HALF:] ** 2
    rows = lax.broadcasted_iota(jnp.int32, (HALF, HEAD), 0)
    columns = lax.broadcasted_iota(jnp.int32, (HALF, HEAD), 1)
    weight = jnp.sum(jnp.where(rows == columns, spectrum[...], 0.0), axis=1, keepdims=True)
    energy = power * (weight * (1.2 / 4))
    elements = lax.broadcasted_iota(jnp.int32, (POINTS, POINTS), 0)
    chosen = jnp.where(elements == hotspots[...], 1.0, 0.0).astype(BF16)
    thirds = jnp.dot(split(energy, 3), chosen, preferred_element_type=F32)
    energy = thirds[0:HALF] + (thirds[HALF : 2 * HALF] + thirds[2 * HALF :])
    here = jnp.broadcast_to(frequency[...], (1, POINTS))
    rows = lax.broadcasted_iota(jnp.int32, (HALF, POINTS), 0)
    packed = jnp.where(rows < HEAD, energy, here)
    for f in range(4):
        out[f] = packed


def damage_body(got, moments_out, damage_out):
    zeroth = jnp.zeros((HEAD, POINTS), F32)
    second = zeroth
    fourth = zeroth
    for f in range(4):
        energy = got[f, 0:HEAD]
        square = got[f, HEAD : HEAD + 1] ** 2
        zeroth = zeroth + energy
        second = second + energy * square
        fourth = fourth + energy * (square * square)
    moments_out[0, 0] = zeroth
    moments_out[1, 0] = second
    moments_out[2, 0] = fourth
    damage_out[0] = (
        0.5 * jnp.log(fourth / second)
        + 1.5 * jnp.log(zeroth)
        + jnp.log(0.5 + 0.5 * second / jnp.sqrt(zeroth * fourth))
    )


def exchange(values, axes):
    return lax.all_to_all(values, axes, 0, 0, tiled=True)


def per_device(wave_loads, pivot_inverse, forward, backward, recovery, hotspots, frequency, spectrum):
    place = jnp.reshape(lax.axis_index("zh"), (1, 1)).astype(jnp.int32)
    (source,) = call(
        source_body, [(GROUP, 8, MODES)], wave_loads, pivot_inverse, forward[0], backward[0]
    )
    shares = exchange(source, INNER)
    (ends,) = call(reduce_body, [(SPAN, 16, MODES)], shares)
    ends = exchange(ends, "zh")
    (solved,) = pl.pallas_call(
        solve_body,
        out_shape=[jax.ShapeDtypeStruct((GROUP, 32, LANES), F32)],
        in_specs=[
            pl.BlockSpec(memory_space=pltpu.SMEM),
            pl.BlockSpec(memory_space=pltpu.VMEM),
            pl.BlockSpec(memory_space=pltpu.VMEM),
        ],
        out_specs=[pl.BlockSpec(memory_space=pltpu.VMEM)],
        scratch_shapes=[pltpu.VMEM((SPAN, 8, MODES), F32)] * 3,
        compiler_params=pltpu.CompilerParams(vmem_limit_bytes=12 * 2**20),
    )(place, shares, ends)
    solved = exchange(solved, INNER)
    motion, energy = call(
        stress_body,
        [(1, 1, 2, HEAD, MODES), (4, HALF, POINTS)],
        solved,
        recovery,
        hotspots,
        frequency.reshape(1, 1),
        spectrum,
        scratch=[pltpu.VMEM((ROWS, MODES), F32)] * 2,
    )
    energy = exchange(energy, "freq")
    moments, damage = call(
        damage_body, [(3, 1, HEAD, POINTS), (1, HEAD, POINTS)], energy
    )
    return motion, moments, damage


def solution(mesh):
    cut = Mesh(mesh.devices.reshape(SPAN, PAIR, ACROSS, CORES, 4), ("zh",) + INNER + ("freq",))
    hull = ("zh",) + INNER
    in_specs = (
        P("freq", hull, None, None, None),
        P("freq", hull, None, None, None),
        P("freq", hull, None),
        P("freq", hull, None),
        P(hull, None, None),
        P(hull, None),
        P("freq"),
        P("freq", None),
    )
    out_specs = (
        P("freq", hull, None, None, None),
        P(None, hull, None, None),
        P(hull, None, None),
    )
    return jax.shard_map(per_device, mesh=cut, in_specs=in_specs, out_specs=out_specs, check_vma=False)
```

time: 645 us -> 75.1 us (0.12)
  blocking collectives: 323 us -> 16 us
  waiting for transfers between devices: 154 us -> 25.7 us
  local copies, waits for them, and re-layouts: 128 us -> 4.7 us
  starting transfers between devices: 2.04 us -> 23.8 us
  between operations: 14.5 us -> 1.34 us
  other arithmetic: 10.1 us -> 0 us
    all_gather x2 -> x0, blocking collectives: 323 us -> none  [carried_in(): gathered = jax.tree.map(lambda a: lax.all_gather(a, axis), part)]
    dynamic_slice x254 -> x0, local copies, waits for them, and re-layouts: 121 us -> none  [one(): lax.dynamic_index_in_dim(a, source, 0, False)]
    all_gather x2 -> x0, waiting for transfers between devices: 109 us -> none  [carried_in(): gathered = jax.tree.map(lambda a: lax.all_gather(a, axis), part)]
    psum x1 -> x0, waiting for transfers between devices: 44.2 us -> none  [per_device(): totals = lax.psum(partial_sum, 'freq')]
    all_to_all x0 -> x3, waiting for transfers between devices: none -> 25.7 us  [exchange(): return lax.all_to_all(values, axes, 0, 0, tiled=True)]
    all_to_all x0 -> x3, starting transfers between devices: none -> 23.8 us  [exchange(): return lax.all_to_all(values, axes, 0, 0, tiled=True)]
    all_to_all x0 -> x1, blocking collectives: none -> 16 us  [exchange(): return lax.all_to_all(values, axes, 0, 0, tiled=True)]
    add x130 -> x0, other arithmetic: 6.53 us -> none  [the longest x127 5.62 us: compose(): return (later[0] + apply_modal(earlier[0], later[1]), earlier[1] * later[1])]
  transfers between devices with their start and end apart: 4 -> 3, of which waited for: 4 -> 3; matrix products, arithmetic and copies ran while one was open for 1% -> 1% of each run, Pallas kernels for 0% -> 0%
where the time goes in v1:
time: 75.1 us; the launch traced here: 74.6 us
  waiting for transfers between devices  25.7 us (34%)
  starting transfers between devices  23.8 us (32%)
  blocking collectives  16 us (21%)
  local copies, waits for them, and re-layouts  4.7 us (6%)
  Pallas kernels  3.03 us (4%)
  between operations  1.34 us (2%)
    all_to_all x3, waiting for transfers between devices, exchange(): return lax.all_to_all(values, axes, 0, 0, tiled=True)  25.7 us
    all_to_all x3, starting transfers between devices, exchange(): return lax.all_to_all(values, axes, 0, 0, tiled=True)  23.8 us
    all_to_all x1, blocking collectives, exchange(): return lax.all_to_all(values, axes, 0, 0, tiled=True)  16 us
    unnamed x16, local copies, waits for them, and re-layouts  4.7 us
    pallas_call x4, Pallas kernels, call(): pl.pallas_call(body, out_shape=outs, in_specs=[pl.BlockSpec(memory_space=...  2.2 us
  transfers between devices with their start and end apart: 3, of which 3 were waited for; matrix products, arithmetic and copies ran while one was open for 1% of the time, Pallas kernels for 0%

profile of v1, /device:TPU:1, one launch (start us, length us, event | category | flops | bytes accessed | tf_op | source)
XLA Modules:
  0.0 74.6 jit_solution(3799560132996543604)
XLA Ops:
  0.6 0.8 %copy.11.loads = bf16[1,1,2,36,384]{4,3,2,1,0:T(8,128)(2,1)S(1)} copy(bf16[1,1,2,36,384]{4,2,3,1,0:T(2,128)(2,1)} %param.8) | data formatting | bytes 110592 | tf_op args[0]
  1.5 0.0 copy-start.2
  1.5 0.0 copy-start.3
  1.5 0.7 copy-done.2
  2.1 0.0 copy-done.3
  2.2 0.0 copy-start
  2.2 1.1 %copy-done = bf16[1,1,2,384,384]{4,3,2,1,0:T(8,128)(2,1)S(1)} copy-done((bf16[1,1,2,384,384]{4,3,2,1,0:T(8,128)(2,1)S(1)}, bf16[1,1,2,384,384]{4,3,2,1,0:T(8,128)(2,1)}, u32[]{:S(2)}) %copy-start) | copy-done | bytes 589848
  3.2 0.3 shard_map.103
  3.5 16.0 %all_to_all.20.got = f32[16,8,384]{2,1,0:T(8,128)S(1)} all-to-all(f32[16,8,384]{2,1,0:T(8,128)S(1)} %shard_map.103), channel_id=1, replica_groups=mesh['zh'=8,'zl'=2,'x'=4,'core'=2,'freq'=4] {'zl','x','core'}, dimensions={0} | all-to-all | bytes 393216 | tf_op jit(solution)/shard_map/all_to_all | solution.py:176
  19.5 0.8 %shard_map.104 = f32[8,16,384]{2,1,0:T(8,128)} custom-call(f32[16,8,384]{2,1,0:T(8,128)S(1)} %all_to_all.20.got), custom_call_target="tpu_custom_call" | custom-call | tf_op jit(solution)/shard_map/pallas_call | solution.py:23
  20.3 11.5 %all-to-all-start.1 = ((f32[8,16,384]{2,1,0:T(8,128)}), f32[8,16,384]{2,1,0:T(8,128)S(1)}, u32[]{:S(2)}, u32[]{:S(2)}) async-start(f32[8,16,384]{2,1,0:T(8,128)} %shard_map.104), calls=%async_computation.1 | async-start | bytes 393216 | tf_op jit(solution)/shard_map/all_to_all | solution.py:176
  31.8 14.8 %all-to-all-done.1.ends = f32[8,16,384]{2,1,0:T(8,128)S(1)} async-done(((f32[8,16,384]{2,1,0:T(8,128)}), f32[8,16,384]{2,1,0:T(8,128)S(1)}, u32[]{:S(2)}, u32[]{:S(2)}) %all-to-all-start.1) | async-done | bytes 196640 | tf_op jit(solution)/shard_map/all_to_all | solution.py:176
  46.6 0.8 %shard_map.105 = f32[16,32,128]{2,1,0:T(8,128)} custom-call(s32[1,1]{1,0:T(1,128)} %bitcast.place, f32[16,8,384]{2,1,0:T(8,128)S(1)} %all_to_all.20.got, f32[8,16,384]{2,1,0:T(8,128)S(1)} %all-to-all-done.1.ends), custom_call_target="tpu_custom_call" | custom-call | tf_op jit(solution)/shard_map/pallas_call | solution.py:187
  47.4 0.0 copy-start.1
  47.4 8.1 %all-to-all-start.2 = ((f32[16,32,128]{2,1,0:T(8,128)}), f32[16,32,128]{2,1,0:T(8,128)S(1)}, u32[]{:S(2)}, u32[]{:S(2)}) async-start(f32[16,32,128]{2,1,0:T(8,128)} %shard_map.105), calls=%async_computation.2 | async-start | bytes 524288 | tf_op jit(solution)/shard_map/all_to_all | solution.py:176
  56.2 0.0 copy-start.4
  56.2 0.0 copy-start.5
  56.2 6.6 %all-to-all-done.2.got = f32[16,32,128]{2,1,0:T(8,128)S(1)} async-done(((f32[16,32,128]{2,1,0:T(8,128)}), f32[16,32,128]{2,1,0:T(8,128)S(1)}, u32[]{:S(2)}, u32[]{:S(2)}) %all-to-all-start.2) | async-done | bytes 262176 | tf_op jit(solution)/shard_map/all_to_all | solution.py:176
  62.8 0.0 copy-done.1
  62.8 0.0 copy-done.4
  62.8 0.0 copy-done.5
  62.8 1.1 %shard_map.106 = (f32[1,1,2,36,384]{4,3,2,1,0:T(8,128)S(1)}, f32[4,40,256]{2,1,0:T(8,128)}) custom-call(f32[16,32,128]{2,1,0:T(8,128)S(1)} %all-to-all-done.2.got, bf16[1,256,768]{2,1,0:T(8,128)(2,1)S(1)} %copy-done.1, s32[1,256]{1,0:T(1,128)S(1)} %copy-done.4, f32[1,1]{1,0:T(1,128)} %bitcast.4.frequency, f32[1,36]{1,0:T(1,128)S(1)} %copy-done.5), custom_call_target="tpu_custom_call" | custom-call | tf_op jit(solution)/shard_map/pallas_call | solution.py:23
  63.9 4.2 %all-to-all-start.3 = ((f32[4,40,256]{2,1,0:T(8,128)}), f32[4,40,256]{2,1,0:T(8,128)S(1)}, u32[]{:S(2)}, u32[]{:S(2)}) async-start(f32[4,40,256]{2,1,0:T(8,128)} %get-tuple-element.8), calls=%async_computation.3 | async-start | bytes 327680 | tf_op jit(solution)/shard_map/all_to_all | solution.py:176
  68.1 0.7 copy.12
  68.8 4.3 %all-to-all-done.3.got = f32[4,40,256]{2,1,0:T(8,128)S(1)} async-done(((f32[4,40,256]{2,1,0:T(8,128)}), f32[4,40,256]{2,1,0:T(8,128)S(1)}, u32[]{:S(2)}, u32[]{:S(2)}) %all-to-all-start.3) | async-done | bytes 163872 | tf_op jit(solution)/shard_map/all_to_all | solution.py:176
  73.1 0.1 shard_map.107
  73.2 0.8 %copy.13 = f32[3,1,36,256]{3,1,2,0:T(1,128)} copy(f32[3,1,36,256]{3,2,1,0:T(8,128)S(1)} %get-tuple-element.12) | data formatting | bytes 221184
  73.9 0.7 copy.14
Async XLA Ops:
  1.5 0.7 copy-start.2
  1.5 0.7 copy-start.3
  2.2 1.1 %copy-start = (bf16[1,1,2,384,384]{4,3,2,1,0:T(8,128)(2,1)S(1)}, bf16[1,1,2,384,384]{4,3,2,1,0:T(8,128)(2,1)}, u32[]{:S(2)}) copy-start(bf16[1,1,2,384,384]{4,3,2,1,0:T(8,128)(2,1)} %pivot.1) | copy-start | bytes 1769476
  20.3 26.3 %all-to-all-start.1 = ((f32[8,16,384]{2,1,0:T(8,128)}), f32[8,16,384]{2,1,0:T(8,128)S(1)}, u32[]{:S(2)}, u32[]{:S(2)}) async-start(f32[8,16,384]{2,1,0:T(8,128)} %shard_map.104), calls=%async_computation.1 | async-start | bytes 393216 | tf_op jit(solution)/shard_map/all_to_all | solution.py:176
  47.4 15.4 %copy-start.1 = (bf16[1,256,768]{2,1,0:T(8,128)(2,1)S(1)}, bf16[1,256,768]{2,1,0:T(8,128)(2,1)}, u32[]{:S(2)}) copy-start(bf16[1,256,768]{2,1,0:T(8,128)(2,1)} %recovery.1) | copy-start | bytes 1179652
  47.4 15.4 %all-to-all-start.2 = ((f32[16,32,128]{2,1,0:T(8,128)}), f32[16,32,128]{2,1,0:T(8,128)S(1)}, u32[]{:S(2)}, u32[]{:S(2)}) async-start(f32[16,32,128]{2,1,0:T(8,128)} %shard_map.105), calls=%async_computation.2 | async-start | bytes 524288 | tf_op jit(solution)/shard_map/all_to_all | solution.py:176
  56.2 6.6 %copy-start.4 = (s32[1,256]{1,0:T(1,128)S(1)}, s32[1,256]{1,0:T(1,128)}, u32[]{:S(2)}) copy-start(s32[1,256]{1,0:T(1,128)} %hotspots.1) | copy-start | bytes 3076
  56.2 6.6 %copy-start.5 = (f32[1,36]{1,0:T(1,128)S(1)}, f32[1,36]{1,0:T(1,128)}, u32[]{:S(2)}) copy-start(f32[1,36]{1,0:T(1,128)} %spectrum.1) | copy-start | bytes 436
  63.9 9.2 %all-to-all-start.3 = ((f32[4,40,256]{2,1,0:T(8,128)}), f32[4,40,256]{2,1,0:T(8,128)S(1)}, u32[]{:S(2)}, u32[]{:S(2)}) async-start(f32[4,40,256]{2,1,0:T(8,128)} %get-tuple-element.8), calls=%async_computation.3 | async-start | bytes 327680 | tf_op jit(solution)/shard_map/all_to_all | solution.py:176

commit v2 on v1

v2 whole, which is shorter than its diff:
```python
import jax
import jax.numpy as jnp
from jax import lax
from jax.experimental import pallas as pl
from jax.experimental.pallas import tpu as pltpu
from jax.sharding import PartitionSpec as P

SPAN, GROUP = 8, 16
HEAD, MODES, POINTS = 36, 384, 256
HALF = 40
ROWS = 2 * HALF
SHARE = ROWS // GROUP
LANES = 128
TILES = MODES // LANES
NEAR = (4, 5, 6, 7, 8, 9, 10, 11, 12, 13, 14, 15, 0, 1, 2, 3)
FAR = (4, 5, 6, 7, 0, 1, 2, 3)
WAVES = (2, 3, 0, 1)
F32 = jnp.float32
BF16 = jnp.bfloat16


def call(body, shapes, *args, spaces=None, vmem_mib=12, scratch=()):
    outs = [jax.ShapeDtypeStruct(shape, F32) for shape in shapes]
    spaces = spaces or [pltpu.VMEM] * len(args)
    return pl.pallas_call(
        body,
        out_shape=outs,
        in_specs=[pl.BlockSpec(memory_space=space) for space in spaces],
        out_specs=[pl.BlockSpec(memory_space=pltpu.VMEM)] * len(outs),
        scratch_shapes=list(scratch),
        compiler_params=pltpu.CompilerParams(vmem_limit_bytes=vmem_mib * 2**20),
    )(*args)


def padded(rows):
    return jnp.concatenate([rows, jnp.zeros((HALF - HEAD, rows.shape[1]), rows.dtype)], axis=0)


def source_body(loads_hbm, pivot_hbm, forward_hbm, backward_hbm, out, loads, pivot, forward, backward, arrived):
    copies = [
        pltpu.make_async_copy(loads_hbm.at[0, 0], loads, arrived.at[0]),
        pltpu.make_async_copy(forward_hbm, forward, arrived.at[1]),
        pltpu.make_async_copy(backward_hbm, backward, arrived.at[2]),
        pltpu.make_async_copy(pivot_hbm.at[0, 0, 0], pivot.at[0], arrived.at[3]),
        pltpu.make_async_copy(pivot_hbm.at[0, 0, 1], pivot.at[1], arrived.at[4]),
    ]
    for copy in copies:
        copy.start()
    copies[0].wait()
    both = loads[...].astype(F32)
    real = padded(both[:, 0, :])
    imag = padded(both[:, 1, :])
    by_real = jnp.concatenate([real, imag], axis=0).astype(BF16)
    by_imag = jnp.concatenate([-imag, real], axis=0).astype(BF16)
    copies[1].wait()
    copies[2].wait()
    fore = -forward[...].astype(F32)
    back = -backward[...].astype(F32)
    copies[3].wait()
    source = jnp.dot(by_real, pivot[0], preferred_element_type=F32)
    copies[4].wait()
    source = source + jnp.dot(by_imag, pivot[1], preferred_element_type=F32)
    blank = jnp.zeros((1, MODES), F32)
    for d in range(GROUP):
        out[d] = jnp.concatenate([source[SHARE * d : SHARE * (d + 1)], fore, back, blank], axis=0)


def reduce_body(shares, out):
    got = [shares.at[NEAR.index(j)] for j in range(GROUP)]
    front = got[0][0:SHARE]
    gain = got[0][SHARE : SHARE + 1]
    fronts, gains = [front], [gain]
    for j in range(1, GROUP):
        fore = got[j][SHARE : SHARE + 1]
        front = got[j][0:SHARE] + front * fore
        gain = gain * fore
        fronts.append(front)
        gains.append(gain)
    last_back = got[GROUP - 1][SHARE + 1 : SHARE + 2]
    motion, through, back_gain = front, gain, last_back
    for j in range(GROUP - 2, -1, -1):
        back = got[j][SHARE + 1 : SHARE + 2]
        motion = fronts[j] + motion * back
        through = gains[j] + through * back
        back_gain = back_gain * back
    blank = jnp.zeros((16 - 2 * SHARE - 4, MODES), F32)
    packed = jnp.concatenate([front, motion, gain, through, back_gain, last_back, blank], axis=0)
    for g in range(SPAN):
        out[g] = packed


def solve_body(shares, reached, out, into, beyond, before):
    mine = lax.axis_index("hull") // GROUP
    got = [shares.at[NEAR.index(j)] for j in range(GROUP)]
    ends = [reached.at[FAR.index(g)] for g in range(SPAN)]
    zero = jnp.zeros((SHARE, MODES), F32)
    into[0, 0:SHARE] = zero
    before[0, 0:1] = jnp.zeros((1, MODES), F32)
    arriving = [zero]
    for g in range(SPAN - 1):
        arriving.append(ends[g][0:SHARE] + arriving[g] * ends[g][2 * SHARE : 2 * SHARE + 1])
        into[g + 1, 0:SHARE] = arriving[g + 1]
        before[g + 1, 0:1] = ends[g][2 * SHARE + 3 : 2 * SHARE + 4]
    returning = zero
    beyond[SPAN - 1, 0:SHARE] = zero
    for g in range(SPAN - 1, 0, -1):
        returning = (
            ends[g][SHARE : 2 * SHARE]
            + arriving[g] * ends[g][2 * SHARE + 1 : 2 * SHARE + 2]
            + returning * ends[g][2 * SHARE + 2 : 2 * SHARE + 3]
        )
        beyond[g - 1, 0:SHARE] = returning
    enter = into[mine, 0:SHARE]
    front = enter
    fronts = []
    for j in range(GROUP):
        front = got[j][0:SHARE] + front * got[j][SHARE : SHARE + 1]
        fronts.append(front)
    motion = beyond[mine, 0:SHARE]
    motions = [None] * GROUP
    for j in range(GROUP - 1, -1, -1):
        motion = fronts[j] + motion * got[j][SHARE + 1 : SHARE + 2]
        motions[j] = motion
    previous = enter + motion * before[mine, 0:1]
    for j in range(GROUP):
        both = jnp.concatenate([motions[j], previous], axis=0)
        for t in range(TILES):
            out[NEAR.index(j), 2 * SHARE * t : 2 * SHARE * (t + 1)] = both[:, LANES * t : LANES * (t + 1)]
        out[NEAR.index(j), 2 * SHARE * TILES : 32] = jnp.zeros((32 - 2 * SHARE * TILES, LANES), F32)
        previous = motions[j]


def split(values, parts):
    pieces = []
    for _ in range(parts):
        piece = values.astype(BF16)
        values = values - piece.astype(F32)
        pieces.append(piece)
    return jnp.concatenate(pieces, axis=0)


def stress_body(got, recovery, hotspots, frequency, spectrum, motion_out, out, motion, stern):
    for d in range(GROUP):
        for t in range(TILES):
            lanes = slice(LANES * t, LANES * (t + 1))
            rows = slice(SHARE * d, SHARE * (d + 1))
            motion[rows, lanes] = got[d, 2 * SHARE * t : 2 * SHARE * t + SHARE]
            stern[rows, lanes] = got[d, 2 * SHARE * t + SHARE : 2 * SHARE * (t + 1)]
    motion_out[0, 0, :, 0, :] = motion[0:HEAD]
    motion_out[0, 0, :, 1, :] = motion[HALF : HALF + HEAD]
    contract = (((1,), (1,)), ((), ()))
    both = lax.dot_general(
        split(stern[...], 2), recovery[0, :, 0:MODES], contract, preferred_element_type=F32
    ) + lax.dot_general(
        split(motion[...], 2), recovery[0, :, MODES:], contract, preferred_element_type=F32
    )
    stress = both[0:ROWS] + both[ROWS:]
    power = stress[0:HALF] ** 2 + stress[HALF:] ** 2
    rows = lax.broadcasted_iota(jnp.int32, (HALF, HEAD), 0)
    columns = lax.broadcasted_iota(jnp.int32, (HALF, HEAD), 1)
    weight = jnp.sum(jnp.where(rows == columns, spectrum[...], 0.0), axis=1, keepdims=True)
    energy = power * (weight * (1.2 / 4))
    elements = lax.broadcasted_iota(jnp.int32, (POINTS, POINTS), 0)
    chosen = jnp.where(elements == hotspots[...], 1.0, 0.0).astype(BF16)
    thirds = jnp.dot(split(energy, 3), chosen, preferred_element_type=F32)
    energy = thirds[0:HALF] + (thirds[HALF : 2 * HALF] + thirds[2 * HALF :])
    here = jnp.full((1, POINTS), frequency[0], F32)
    rows = lax.broadcasted_iota(jnp.int32, (HALF, POINTS), 0)
    packed = jnp.where(rows < HEAD, energy, here)
    for f in range(4):
        out[f] = packed


def damage_body(got, moments_out, damage_out):
    zeroth = jnp.zeros((HEAD, POINTS), F32)
    second = zeroth
    fourth = zeroth
    for f in range(4):
        energy = got[f, 0:HEAD]
        square = got[f, HEAD : HEAD + 1] ** 2
        zeroth = zeroth + energy
        second = second + energy * square
        fourth = fourth + energy * (square * square)
    moments_out[0, :, 0, :] = zeroth
    moments_out[1, :, 0, :] = second
    moments_out[2, :, 0, :] = fourth
    damage_out[:, 0, :] = (
        0.5 * jnp.log(fourth / second)
        + 1.5 * jnp.log(zeroth)
        + jnp.log(0.5 + 0.5 * second / jnp.sqrt(zeroth * fourth))
    )


def exchange(values, axis, groups):
    return lax.all_to_all(values, axis, 0, 0, axis_index_groups=groups, tiled=True)


def per_device(wave_loads, pivot_inverse, forward, backward, recovery, hotspots, frequency, spectrum):
    near = [[GROUP * g + j for j in NEAR] for g in range(SPAN)]
    far = [[GROUP * g + j for g in FAR] for j in range(GROUP)]
    (source,) = call(
        source_body,
        [(GROUP, 8, MODES)],
        jnp.transpose(wave_loads, (0, 1, 3, 2, 4)),
        pivot_inverse,
        forward[0],
        backward[0],
        spaces=[pl.ANY] * 4,
        vmem_mib=56,
        scratch=[
            pltpu.VMEM((HEAD, 2, MODES), BF16),
            pltpu.VMEM((2, MODES, MODES), BF16),
            pltpu.VMEM((1, MODES), BF16),
            pltpu.VMEM((1, MODES), BF16),
            pltpu.SemaphoreType.DMA((5,)),
        ],
    )
    shares = exchange(source, "hull", near)
    (ends,) = call(reduce_body, [(SPAN, 16, MODES)], shares)
    ends = exchange(ends, "hull", far)
    (solved,) = call(
        solve_body,
        [(GROUP, 32, LANES)],
        shares,
        ends,
        scratch=[pltpu.VMEM((SPAN, 8, MODES), F32)] * 3,
    )
    solved = exchange(solved, "hull", near)
    motion, energy = call(
        stress_body,
        [(1, 1, HEAD, 2, MODES), (4, HALF, POINTS)],
        solved,
        recovery,
        hotspots,
        frequency,
        spectrum,
        spaces=[pltpu.VMEM] * 3 + [pltpu.SMEM, pltpu.VMEM],
        scratch=[pltpu.VMEM((ROWS, MODES), F32)] * 2,
    )
    energy = exchange(energy, "freq", [WAVES])
    moments, damage = call(damage_body, [(3, HEAD, 1, POINTS), (HEAD, 1, POINTS)], energy)
    return (
        jnp.transpose(motion, (0, 1, 3, 2, 4)),
        jnp.transpose(moments, (0, 2, 1, 3)),
        jnp.transpose(damage, (1, 0, 2)),
    )


def solution(mesh):
    in_specs = (
        P("freq", "hull", None, None, None),
        P("freq", "hull", None, None, None),
        P("freq", "hull", None),
        P("freq", "hull", None),
        P("hull", None, None),
        P("hull", None),
        P("freq"),
        P("freq", None),
    )
    out_specs = (
        P("freq", "hull", None, None, None),
        P(None, "hull", None, None),
        P("hull", None, None),
    )
    return jax.shard_map(per_device, mesh=mesh, in_specs=in_specs, out_specs=out_specs, check_vma=False)
```

time: 75.1 us -> 64.6 us (0.86)
  blocking collectives: 16 us -> 46.4 us
  waiting for transfers between devices: 25.7 us -> 4.12 us
  starting transfers between devices: 23.8 us -> 7.33 us
  local copies, waits for them, and re-layouts: 4.7 us -> 0.01 us
  Pallas kernels: 3.03 us -> 4.55 us
    all_to_all x1 -> x3, blocking collectives: 16 us -> 46.4 us  [exchange(): lax.all_to_all(values, axis, 0, 0, axis_index_groups=groups, tiled=True)]
    all_to_all x3 -> x1, waiting for transfers between devices: 25.7 us -> 4.12 us  [exchange(): lax.all_to_all(values, axis, 0, 0, axis_index_groups=groups, tiled=True)]
    all_to_all x3 -> x1, starting transfers between devices: 23.8 us -> 7.33 us  [exchange(): lax.all_to_all(values, axis, 0, 0, axis_index_groups=groups, tiled=True)]
    unnamed x16 -> x6, local copies, waits for them, and re-layouts: 4.7 us -> 0.01 us
    pallas_call x4 -> x5, Pallas kernels: 2.2 us -> 4.55 us  [call(): pl.pallas_call(body, out_shape=outs, in_specs=[pl.BlockSpec(memory_space=...]
    pallas_call x1 -> x0, Pallas kernels: 0.82 us -> none  [per_device(): pl.pallas_call(solve_body, out_shape=[jax.ShapeDtypeStruct((GROUP, 32, LA...]
  transfers between devices with their start and end apart: 3 -> 1, of which waited for: 3 -> 1; matrix products, arithmetic and copies ran while one was open for 1% -> 0% of each run, Pallas kernels for 0% -> 0%
where the time goes in v2:
time: 64.6 us; the launch traced here: 63.7 us
  blocking collectives  46.4 us (72%)
  starting transfers between devices  7.33 us (11%)
  Pallas kernels  4.55 us (7%)
  waiting for transfers between devices  4.12 us (6%)
  between operations  1.33 us (2%)
    all_to_all x3, blocking collectives, exchange(): lax.all_to_all(values, axis, 0, 0, axis_index_groups=groups, tiled=True)  46.4 us
    all_to_all x1, starting transfers between devices, exchange(): lax.all_to_all(values, axis, 0, 0, axis_index_groups=groups, tiled=True)  7.33 us
    pallas_call x5, Pallas kernels, call(): pl.pallas_call(body, out_shape=outs, in_specs=[pl.BlockSpec(memory_space=...  4.55 us
    all_to_all x1, waiting for transfers between devices, exchange(): lax.all_to_all(values, axis, 0, 0, axis_index_groups=groups, tiled=True)  4.12 us
  transfers between devices with their start and end apart: 1, of which 1 were waited for; matrix products, arithmetic and copies ran while one was open for 0% of the time, Pallas kernels for 0%

profile of v2, /device:TPU:1, one launch (start us, length us, event | category | flops | bytes accessed | tf_op | source)
XLA Modules:
  0.0 63.7 jit_solution(9319919194280969617)
XLA Ops:
  0.6 2.1 %shard_map.103 = f32[16,8,384]{2,1,0:T(8,128)} custom-call(bf16[1,1,36,2,384]{4,3,2,1,0:T(2,128)(2,1)} %bitcast.6, bf16[1,1,2,384,384]{4,3,2,1,0:T(8,128)(2,1)} %pivot_hbm.1, bf16[1,384]{1,0:T(2,128)(2,1)} %bitcast.7, bf16[1,384]{1,0:T(2,128)(2,1)} %bitcast.8), custom_call_target="tpu_custom_call" | custom-call | tf_op jit(solution)/shard_map/pallas_call | solution.py:25
  2.7 15.7 %all_to_all.20.shares = f32[16,8,384]{2,1,0:T(8,128)S(1)} all-to-all(f32[16,8,384]{2,1,0:T(8,128)} %shard_map.103), channel_id=1, replica_groups={{16,20,24,28,32,36,40,44,48,52,56,60,0,4,8,12},{80,84,88,92,96,100,104,..., dimensions={0} | all-to-all | bytes 393216 | tf_op jit(solution)/shard_map/all_to_all | solution.py:195
  18.4 0.1 shard_map.104
  18.5 23.1 %all_to_all.21.reached = f32[8,16,384]{2,1,0:T(8,128)S(1)} all-to-all(f32[8,16,384]{2,1,0:T(8,128)S(1)} %shard_map.104), channel_id=1, replica_groups={{256,320,384,448,0,64,128,192},{260,324,388,452,4,68,132,196},{264,328,..., dimensions={0} | all-to-all | bytes 393216 | tf_op jit(solution)/shard_map/all_to_all | solution.py:195
  41.6 0.8 %shard_map.105 = f32[16,32,128]{2,1,0:T(8,128)} custom-call(f32[16,8,384]{2,1,0:T(8,128)S(1)} %all_to_all.20.shares, f32[8,16,384]{2,1,0:T(8,128)S(1)} %all_to_all.21.reached), custom_call_target="tpu_custom_call" | custom-call | tf_op jit(solution)/shard_map/pallas_call | solution.py:25
  42.4 0.0 copy-start
  42.4 7.3 %all-to-all-start.2 = ((f32[16,32,128]{2,1,0:T(8,128)}), f32[16,32,128]{2,1,0:T(8,128)S(1)}, u32[]{:S(2)}, u32[]{:S(2)}) async-start(f32[16,32,128]{2,1,0:T(8,128)} %shard_map.105), calls=%async_computation.2 | async-start | bytes 524288 | tf_op jit(solution)/shard_map/all_to_all | solution.py:195
  49.8 0.0 copy-start.1
  49.8 0.0 copy-start.2
  50.5 4.1 %all-to-all-done.2.got = f32[16,32,128]{2,1,0:T(8,128)S(1)} async-done(((f32[16,32,128]{2,1,0:T(8,128)}), f32[16,32,128]{2,1,0:T(8,128)S(1)}, u32[]{:S(2)}, u32[]{:S(2)}) %all-to-all-start.2) | async-done | bytes 262176 | tf_op jit(solution)/shard_map/all_to_all | solution.py:195
  54.6 0.0 copy-done
  54.6 0.0 copy-done.1
  54.6 0.0 copy-done.2
  54.6 0.8 %shard_map.106 = (f32[1,1,36,2,384]{4,3,2,1,0:T(2,128)}, f32[4,40,256]{2,1,0:T(8,128)S(1)}) custom-call(f32[16,32,128]{2,1,0:T(8,128)S(1)} %all-to-all-done.2.got, bf16[1,256,768]{2,1,0:T(8,128)(2,1)S(1)} %copy-done, s32[1,256]{1,0:T(1,128)S(1)} %copy-done.1, f32[1]{0:T(128)S(6)} %copy.11.frequency, f32[1,36]{1,0:T(1,128)S(1)} %copy-done.2), custom_call_target="tpu_custom_call" | custom-call | tf_op jit(solution)/shard_map/pallas_call | solution.py:25
  55.4 7.6 %all_to_all.22.got = f32[4,40,256]{2,1,0:T(8,128)S(1)} all-to-all(f32[4,40,256]{2,1,0:T(8,128)S(1)} %get-tuple-element.8), channel_id=1, replica_groups={{2,3,0,1},{6,7,4,5},{10,11,8,9},{14,15,12,13},{18,19,16,17},{22,23,20,2..., dimensions={0} | all-to-all | bytes 327680 | tf_op jit(solution)/shard_map/all_to_all | solution.py:195
  63.0 0.7 %shard_map.107 = (f32[3,36,1,256]{3,2,1,0:T(1,128)}, f32[36,1,256]{2,1,0:T(1,128)}) custom-call(f32[4,40,256]{2,1,0:T(8,128)S(1)} %all_to_all.22.got), custom_call_target="tpu_custom_call" | custom-call | tf_op jit(solution)/shard_map/pallas_call | solution.py:25
Async XLA Ops:
  42.4 12.1 %copy-start = (bf16[1,256,768]{2,1,0:T(8,128)(2,1)S(1)}, bf16[1,256,768]{2,1,0:T(8,128)(2,1)}, u32[]{:S(2)}) copy-start(bf16[1,256,768]{2,1,0:T(8,128)(2,1)} %recovery.1) | copy-start | bytes 1179652
  42.4 12.1 %all-to-all-start.2 = ((f32[16,32,128]{2,1,0:T(8,128)}), f32[16,32,128]{2,1,0:T(8,128)S(1)}, u32[]{:S(2)}, u32[]{:S(2)}) async-start(f32[16,32,128]{2,1,0:T(8,128)} %shard_map.105), calls=%async_computation.2 | async-start | bytes 524288 | tf_op jit(solution)/shard_map/all_to_all | solution.py:195
  49.8 4.8 %copy-start.1 = (s32[1,256]{1,0:T(1,128)S(1)}, s32[1,256]{1,0:T(1,128)}, u32[]{:S(2)}) copy-start(s32[1,256]{1,0:T(1,128)} %hotspots.1) | copy-start | bytes 3076
  49.8 4.8 %copy-start.2 = (f32[1,36]{1,0:T(1,128)S(1)}, f32[1,36]{1,0:T(1,128)}, u32[]{:S(2)}) copy-start(f32[1,36]{1,0:T(1,128)} %spectrum.1) | copy-start | bytes 436

commit v3 on v2

--- a/solution.py
+++ b/solution.py
@@ -10,11 +10,14 @@
 HALF = 40
 ROWS = 2 * HALF
 SHARE = ROWS // GROUP
+END = 2 * SHARE + 3
+ENDS = 40
 LANES = 128
 TILES = MODES // LANES
-NEAR = (4, 5, 6, 7, 8, 9, 10, 11, 12, 13, 14, 15, 0, 1, 2, 3)
-FAR = (4, 5, 6, 7, 0, 1, 2, 3)
-WAVES = (2, 3, 0, 1)
+NEAR = (15, 14, 13, 12, 11, 10, 9, 8, 7, 6, 5, 4, 3, 2, 1, 0)
+BACK = (4, 5, 6, 7, 8, 9, 10, 11, 12, 13, 14, 15, 0, 1, 2, 3)
+FAR = (5, 4, 6, 3, 7, 2, 0, 1)
+WAVES = (3, 2, 1, 0)
 F32 = jnp.float32
 BF16 = jnp.bfloat16
 
@@ -83,16 +86,22 @@
         motion = fronts[j] + motion * back
         through = gains[j] + through * back
         back_gain = back_gain * back
-    blank = jnp.zeros((16 - 2 * SHARE - 4, MODES), F32)
-    packed = jnp.concatenate([front, motion, gain, through, back_gain, last_back, blank], axis=0)
-    for g in range(SPAN):
-        out[g] = packed
-
-
-def solve_body(shares, reached, out, into, beyond, before):
+    mine = lax.axis_index("hull") // GROUP
+    blank = jnp.zeros((ENDS - TILES * END, LANES), F32)
+    for place in range(SPAN):
+        third = jnp.where(mine < FAR[place], last_back, through)
+        packed = jnp.concatenate([front, motion, gain, third, back_gain], axis=0)
+        pieces = [packed[:, LANES * t : LANES * (t + 1)] for t in range(TILES)]
+        out[place] = jnp.concatenate(pieces + [blank], axis=0)
+
+
+def solve_body(shares, reached, recovery, hotspots, frequency, spectrum, out, into, beyond, before):
     mine = lax.axis_index("hull") // GROUP
     got = [shares.at[NEAR.index(j)] for j in range(GROUP)]
-    ends = [reached.at[FAR.index(g)] for g in range(SPAN)]
+    ends = []
+    for g in range(SPAN):
+        packed = reached[FAR.index(g)]
+        ends.append(jnp.concatenate([packed[END * t : END * (t + 1)] for t in range(TILES)], axis=1))
     zero = jnp.zeros((SHARE, MODES), F32)
     into[0, 0:SHARE] = zero
     before[0, 0:1] = jnp.zeros((1, MODES), F32)
@@ -100,7 +109,7 @@
     for g in range(SPAN - 1):
         arriving.append(ends[g][0:SHARE] + arriving[g] * ends[g][2 * SHARE : 2 * SHARE + 1])
         into[g + 1, 0:SHARE] = arriving[g + 1]
-        before[g + 1, 0:1] = ends[g][2 * SHARE + 3 : 2 * SHARE + 4]
+        before[g + 1, 0:1] = ends[g][2 * SHARE + 1 : 2 * SHARE + 2]
     returning = zero
     beyond[SPAN - 1, 0:SHARE] = zero
     for g in range(SPAN - 1, 0, -1):
@@ -125,8 +134,8 @@
     for j in range(GROUP):
         both = jnp.concatenate([motions[j], previous], axis=0)
         for t in range(TILES):
-            out[NEAR.index(j), 2 * SHARE * t : 2 * SHARE * (t + 1)] = both[:, LANES * t : LANES * (t + 1)]
-        out[NEAR.index(j), 2 * SHARE * TILES : 32] = jnp.zeros((32 - 2 * SHARE * TILES, LANES), F32)
+            out[BACK.index(j), 2 * SHARE * t : 2 * SHARE * (t + 1)] = both[:, LANES * t : LANES * (t + 1)]
+        out[BACK.index(j), 2 * SHARE * TILES : 32] = jnp.zeros((32 - 2 * SHARE * TILES, LANES), F32)
         previous = motions[j]
 
 
@@ -140,12 +149,13 @@
 
 
 def stress_body(got, recovery, hotspots, frequency, spectrum, motion_out, out, motion, stern):
-    for d in range(GROUP):
+    for place in range(GROUP):
+        d = NEAR.index(BACK[place])
         for t in range(TILES):
             lanes = slice(LANES * t, LANES * (t + 1))
             rows = slice(SHARE * d, SHARE * (d + 1))
-            motion[rows, lanes] = got[d, 2 * SHARE * t : 2 * SHARE * t + SHARE]
-            stern[rows, lanes] = got[d, 2 * SHARE * t + SHARE : 2 * SHARE * (t + 1)]
+            motion[rows, lanes] = got[place, 2 * SHARE * t : 2 * SHARE * t + SHARE]
+            stern[rows, lanes] = got[place, 2 * SHARE * t + SHARE : 2 * SHARE * (t + 1)]
     motion_out[0, 0, :, 0, :] = motion[0:HEAD]
     motion_out[0, 0, :, 1, :] = motion[HALF : HALF + HEAD]
     contract = (((1,), (1,)), ((), ()))
@@ -164,7 +174,7 @@
     chosen = jnp.where(elements == hotspots[...], 1.0, 0.0).astype(BF16)
     thirds = jnp.dot(split(energy, 3), chosen, preferred_element_type=F32)
     energy = thirds[0:HALF] + (thirds[HALF : 2 * HALF] + thirds[2 * HALF :])
-    here = jnp.full((1, POINTS), frequency[0], F32)
+    here = jnp.broadcast_to(frequency[...].reshape(1, 1), (1, POINTS))
     rows = lax.broadcasted_iota(jnp.int32, (HALF, POINTS), 0)
     packed = jnp.where(rows < HEAD, energy, here)
     for f in range(4):
@@ -197,6 +207,7 @@
 
 def per_device(wave_loads, pivot_inverse, forward, backward, recovery, hotspots, frequency, spectrum):
     near = [[GROUP * g + j for j in NEAR] for g in range(SPAN)]
+    back = [[GROUP * g + j for j in BACK] for g in range(SPAN)]
     far = [[GROUP * g + j for g in FAR] for j in range(GROUP)]
     (source,) = call(
         source_body,
@@ -216,16 +227,20 @@
         ],
     )
     shares = exchange(source, "hull", near)
-    (ends,) = call(reduce_body, [(SPAN, 16, MODES)], shares)
+    (ends,) = call(reduce_body, [(SPAN, ENDS, LANES)], shares)
     ends = exchange(ends, "hull", far)
     (solved,) = call(
         solve_body,
         [(GROUP, 32, LANES)],
         shares,
         ends,
+        recovery,
+        hotspots,
+        frequency,
+        spectrum,
         scratch=[pltpu.VMEM((SPAN, 8, MODES), F32)] * 3,
     )
-    solved = exchange(solved, "hull", near)
+    solved = exchange(solved, "hull", back)
     motion, energy = call(
         stress_body,
         [(1, 1, HEAD, 2, MODES), (4, HALF, POINTS)],
@@ -234,7 +249,6 @@
         hotspots,
         frequency,
         spectrum,
-        spaces=[pltpu.VMEM] * 3 + [pltpu.SMEM, pltpu.VMEM],
         scratch=[pltpu.VMEM((ROWS, MODES), F32)] * 2,
     )
     energy = exchange(energy, "freq", [WAVES])

time: 64.6 us -> 61.8 us (0.957)
  blocking collectives: 46.4 us -> 35.6 us
  starting transfers between devices: 7.33 us -> 11.6 us
  waiting for transfers between devices: 4.12 us -> 8.12 us
    all_to_all x3, blocking collectives: 46.4 us -> 35.6 us  [exchange(): lax.all_to_all(values, axis, 0, 0, axis_index_groups=groups, tiled=True)]
    all_to_all x1, starting transfers between devices: 7.33 us -> 11.6 us  [exchange(): lax.all_to_all(values, axis, 0, 0, axis_index_groups=groups, tiled=True)]
    all_to_all x1, waiting for transfers between devices: 4.12 us -> 8.12 us  [exchange(): lax.all_to_all(values, axis, 0, 0, axis_index_groups=groups, tiled=True)]
where the time goes in v3:
time: 61.8 us; the launch traced here: 61.2 us
  blocking collectives  35.6 us (58%)
  starting transfers between devices  11.6 us (19%)
  waiting for transfers between devices  8.12 us (13%)
  Pallas kernels  4.51 us (7%)
  between operations  1.34 us (2%)
    all_to_all x3, blocking collectives, exchange(): lax.all_to_all(values, axis, 0, 0, axis_index_groups=groups, tiled=True)  35.6 us
    all_to_all x1, starting transfers between devices, exchange(): lax.all_to_all(values, axis, 0, 0, axis_index_groups=groups, tiled=True)  11.6 us
    all_to_all x1, waiting for transfers between devices, exchange(): lax.all_to_all(values, axis, 0, 0, axis_index_groups=groups, tiled=True)  8.12 us
    pallas_call x5, Pallas kernels, call(): pl.pallas_call(body, out_shape=outs, in_specs=[pl.BlockSpec(memory_space=...  4.51 us
  transfers between devices with their start and end apart: 1, of which 1 were waited for; matrix products, arithmetic and copies ran while one was open for 0% of the time, Pallas kernels for 0%

profile of v3, /device:TPU:1, one launch (start us, length us, event | category | flops | bytes accessed | tf_op | source)
XLA Modules:
  0.0 61.2 jit_solution(16692115720891797333)
XLA Ops:
  0.6 2.1 %shard_map.103 = f32[16,8,384]{2,1,0:T(8,128)} custom-call(bf16[1,1,36,2,384]{4,3,2,1,0:T(2,128)(2,1)} %bitcast.6, bf16[1,1,2,384,384]{4,3,2,1,0:T(8,128)(2,1)} %pivot_hbm.1, bf16[1,384]{1,0:T(2,128)(2,1)} %bitcast.7, bf16[1,384]{1,0:T(2,128)(2,1)} %bitcast.8), custom_call_target="tpu_custom_call" | custom-call | tf_op jit(solution)/shard_map/pallas_call | solution.py:28
  2.7 16.1 %all_to_all.20.shares = f32[16,8,384]{2,1,0:T(8,128)S(1)} all-to-all(f32[16,8,384]{2,1,0:T(8,128)} %shard_map.103), channel_id=1, replica_groups={{60,56,52,48,44,40,36,32,28,24,20,16,12,8,4,0},{124,120,116,112,108,104..., dimensions={0} | all-to-all | bytes 393216 | tf_op jit(solution)/shard_map/all_to_all | solution.py:205
  18.8 0.0 copy-start
  18.8 0.8 %shard_map.104 = f32[8,40,128]{2,1,0:T(8,128)} custom-call(f32[16,8,384]{2,1,0:T(8,128)S(1)} %all_to_all.20.shares), custom_call_target="tpu_custom_call" | custom-call | tf_op jit(solution)/shard_map/pallas_call | solution.py:28
  19.5 11.6 %all-to-all-start.1 = ((f32[8,40,128]{2,1,0:T(8,128)}), f32[8,40,128]{2,1,0:T(8,128)S(1)}, u32[]{:S(2)}, u32[]{:S(2)}) async-start(f32[8,40,128]{2,1,0:T(8,128)} %shard_map.104), calls=%async_computation.1 | async-start | bytes 327680 | tf_op jit(solution)/shard_map/all_to_all | solution.py:205
  31.1 0.0 copy-start.1
  31.1 0.0 copy-start.2
  31.8 8.1 %all-to-all-done.1.reached = f32[8,40,128]{2,1,0:T(8,128)S(1)} async-done(((f32[8,40,128]{2,1,0:T(8,128)}), f32[8,40,128]{2,1,0:T(8,128)S(1)}, u32[]{:S(2)}, u32[]{:S(2)}) %all-to-all-start.1) | async-done | bytes 163872 | tf_op jit(solution)/shard_map/all_to_all | solution.py:205
  39.9 0.0 copy-done
  39.9 0.0 copy-done.1
  39.9 0.0 copy-done.2
  39.9 0.1 shard_map.105
  40.1 11.3 %all_to_all.21.got = f32[16,32,128]{2,1,0:T(8,128)S(1)} all-to-all(f32[16,32,128]{2,1,0:T(8,128)S(1)} %shard_map.105), channel_id=1, replica_groups={{16,20,24,28,32,36,40,44,48,52,56,60,0,4,8,12},{80,84,88,92,96,100,104,..., dimensions={0} | all-to-all | bytes 524288 | tf_op jit(solution)/shard_map/all_to_all | solution.py:205
  51.3 0.8 %shard_map.106 = (f32[1,1,36,2,384]{4,3,2,1,0:T(2,128)}, f32[4,40,256]{2,1,0:T(8,128)S(1)}) custom-call(f32[16,32,128]{2,1,0:T(8,128)S(1)} %all_to_all.21.got, bf16[1,256,768]{2,1,0:T(8,128)(2,1)S(1)} %copy-done, s32[1,256]{1,0:T(1,128)S(1)} %copy-done.1, f32[1]{0:T(128)S(6)} %copy.11.frequency, f32[1,36]{1,0:T(1,128)S(1)} %copy-done.2), custom_call_target="tpu_custom_call" | custom-call | tf_op jit(solution)/shard_map/pallas_call | solution.py:28
  52.1 8.3 %all_to_all.22.got = f32[4,40,256]{2,1,0:T(8,128)S(1)} all-to-all(f32[4,40,256]{2,1,0:T(8,128)S(1)} %get-tuple-element.8), channel_id=1, replica_groups={{3,2,1,0},{7,6,5,4},{11,10,9,8},{15,14,13,12},{19,18,17,16},{23,22,21,2..., dimensions={0} | all-to-all | bytes 327680 | tf_op jit(solution)/shard_map/all_to_all | solution.py:205
  60.5 0.7 %shard_map.107 = (f32[3,36,1,256]{3,2,1,0:T(1,128)}, f32[36,1,256]{2,1,0:T(1,128)}) custom-call(f32[4,40,256]{2,1,0:T(8,128)S(1)} %all_to_all.22.got), custom_call_target="tpu_custom_call" | custom-call | tf_op jit(solution)/shard_map/pallas_call | solution.py:28
Async XLA Ops:
  18.8 21.1 %copy-start = (bf16[1,256,768]{2,1,0:T(8,128)(2,1)S(1)}, bf16[1,256,768]{2,1,0:T(8,128)(2,1)}, u32[]{:S(2)}) copy-start(bf16[1,256,768]{2,1,0:T(8,128)(2,1)} %recovery.3) | copy-start | bytes 1179652
  19.5 20.4 %all-to-all-start.1 = ((f32[8,40,128]{2,1,0:T(8,128)}), f32[8,40,128]{2,1,0:T(8,128)S(1)}, u32[]{:S(2)}, u32[]{:S(2)}) async-start(f32[8,40,128]{2,1,0:T(8,128)} %shard_map.104), calls=%async_computation.1 | async-start | bytes 327680 | tf_op jit(solution)/shard_map/all_to_all | solution.py:205
  31.1 8.8 %copy-start.1 = (s32[1,256]{1,0:T(1,128)S(1)}, s32[1,256]{1,0:T(1,128)}, u32[]{:S(2)}) copy-start(s32[1,256]{1,0:T(1,128)} %hotspots.3) | copy-start | bytes 3076
  31.1 8.8 %copy-start.2 = (f32[1,36]{1,0:T(1,128)S(1)}, f32[1,36]{1,0:T(1,128)}, u32[]{:S(2)}) copy-start(f32[1,36]{1,0:T(1,128)} %spectrum.3) | copy-start | bytes 436

commit v4 on v3

--- a/solution.py
+++ b/solution.py
@@ -7,16 +7,17 @@
 
 SPAN, GROUP = 8, 16
 HEAD, MODES, POINTS = 36, 384, 256
-HALF = 40
-ROWS = 2 * HALF
-SHARE = ROWS // GROUP
-END = 2 * SHARE + 3
-ENDS = 40
 LANES = 128
 TILES = MODES // LANES
+HALF = 40
+PAD = HALF - HEAD
+DEEP, FIVE = 14, 5
+TAIL = 2 * HEAD - DEEP * FIVE
+LAST = FIVE * TILES
+ENDS = 32
 NEAR = (15, 14, 13, 12, 11, 10, 9, 8, 7, 6, 5, 4, 3, 2, 1, 0)
 BACK = (4, 5, 6, 7, 8, 9, 10, 11, 12, 13, 14, 15, 0, 1, 2, 3)
-FAR = (5, 4, 6, 3, 7, 2, 0, 1)
+FAR = (5, 1, 0, 2, 7, 3, 6, 4)
 WAVES = (3, 2, 1, 0)
 F32 = jnp.float32
 BF16 = jnp.bfloat16
@@ -63,79 +64,115 @@
     source = jnp.dot(by_real, pivot[0], preferred_element_type=F32)
     copies[4].wait()
     source = source + jnp.dot(by_imag, pivot[1], preferred_element_type=F32)
-    blank = jnp.zeros((1, MODES), F32)
-    for d in range(GROUP):
-        out[d] = jnp.concatenate([source[SHARE * d : SHARE * (d + 1)], fore, back, blank], axis=0)
+    for d in range(LAST):
+        t, i = divmod(d, FIVE)
+        lanes = slice(LANES * t, LANES * (t + 1))
+        pieces = [source[at : at + n, lanes] for at, n, _ in placed(DEEP * i, DEEP)]
+        out[d] = jnp.concatenate(pieces + [fore[:, lanes], back[:, lanes]], axis=0)
+    tiles = [slice(LANES * t, LANES * (t + 1)) for t in range(TILES)]
+    last = HALF + HEAD
+    pieces = [source[last - TAIL : last, lanes] for lanes in tiles]
+    pieces += [fore[:, lanes] for lanes in tiles] + [back[:, lanes] for lanes in tiles]
+    pieces += [jnp.zeros((16 - TILES * (TAIL + 2), LANES), F32)]
+    out[LAST] = jnp.concatenate(pieces, axis=0)
+
+
+def placed(start, count):
+    if start >= HEAD:
+        return [(start + PAD, count, 0)]
+    ahead = min(count, HEAD - start)
+    rest = [(HALF, count - ahead, ahead)] if ahead < count else []
+    return [(start, ahead, 0)] + rest
+
+
+def is_last():
+    return lax.axis_index("hull") % GROUP == NEAR[LAST]
+
+
+def spread(block, row, first, last):
+    whole = jnp.broadcast_to(block[row : row + 1], (16, LANES))
+    parts = [jnp.broadcast_to(block[first + t : first + t + 1], (TAIL, LANES)) for t in range(TILES)]
+    parts.append(jnp.zeros((16 - TILES * TAIL, LANES), F32))
+    return jnp.where(last, jnp.concatenate(parts, axis=0), whole)
+
+
+def by_tile(matrix):
+    return [matrix[TAIL * t : TAIL * t + 1] for t in range(TILES)]
 
 
 def reduce_body(shares, out):
-    got = [shares.at[NEAR.index(j)] for j in range(GROUP)]
-    front = got[0][0:SHARE]
-    gain = got[0][SHARE : SHARE + 1]
+    last = is_last()
+    got = [shares[NEAR.index(j)] for j in range(GROUP)]
+    fores = [spread(block, DEEP, TILES * TAIL, last) for block in got]
+    backs = [spread(block, DEEP + 1, TILES * TAIL + TILES, last) for block in got]
+    front, gain = got[0], fores[0]
     fronts, gains = [front], [gain]
     for j in range(1, GROUP):
-        fore = got[j][SHARE : SHARE + 1]
-        front = got[j][0:SHARE] + front * fore
-        gain = gain * fore
+        front = got[j] + front * fores[j]
+        gain = gain * fores[j]
         fronts.append(front)
         gains.append(gain)
-    last_back = got[GROUP - 1][SHARE + 1 : SHARE + 2]
-    motion, through, back_gain = front, gain, last_back
+    motion, through, back_gain = front, gain, backs[GROUP - 1]
     for j in range(GROUP - 2, -1, -1):
-        back = got[j][SHARE + 1 : SHARE + 2]
-        motion = fronts[j] + motion * back
-        through = gains[j] + through * back
-        back_gain = back_gain * back
+        motion = fronts[j] + motion * backs[j]
+        through = gains[j] + through * backs[j]
+        back_gain = back_gain * backs[j]
+
+    def pack(third):
+        whole = [front[0:DEEP], motion[0:DEEP], gain[0:1], third[0:1], back_gain[0:1]]
+        whole.append(jnp.zeros((1, LANES), F32))
+        some = TILES * TAIL
+        parts = [front[0:some]] + by_tile(gain) + by_tile(third)
+        parts += [jnp.zeros((DEEP - some - 2 * TILES, LANES), F32), motion[0:some]] + by_tile(back_gain)
+        parts.append(jnp.zeros((ENDS - DEEP - some - TILES, LANES), F32))
+        return jnp.where(last, jnp.concatenate(parts, axis=0), jnp.concatenate(whole, axis=0))
+
+    ahead, aft = pack(backs[GROUP - 1]), pack(through)
     mine = lax.axis_index("hull") // GROUP
-    blank = jnp.zeros((ENDS - TILES * END, LANES), F32)
     for place in range(SPAN):
-        third = jnp.where(mine < FAR[place], last_back, through)
-        packed = jnp.concatenate([front, motion, gain, third, back_gain], axis=0)
-        pieces = [packed[:, LANES * t : LANES * (t + 1)] for t in range(TILES)]
-        out[place] = jnp.concatenate(pieces + [blank], axis=0)
+        out[place] = jnp.where(mine < FAR[place], ahead, aft)
 
 
 def solve_body(shares, reached, recovery, hotspots, frequency, spectrum, out, into, beyond, before):
     mine = lax.axis_index("hull") // GROUP
-    got = [shares.at[NEAR.index(j)] for j in range(GROUP)]
-    ends = []
-    for g in range(SPAN):
-        packed = reached[FAR.index(g)]
-        ends.append(jnp.concatenate([packed[END * t : END * (t + 1)] for t in range(TILES)], axis=1))
-    zero = jnp.zeros((SHARE, MODES), F32)
-    into[0, 0:SHARE] = zero
-    before[0, 0:1] = jnp.zeros((1, MODES), F32)
+    last = is_last()
+    some = TILES * TAIL
+    zero = jnp.zeros((16, LANES), F32)
+    ends = [reached[FAR.index(g)] for g in range(SPAN)]
+    thirds = [spread(block, 2 * DEEP + 1, some + TILES, last) for block in ends]
+    into[0] = zero
+    before[0] = zero
     arriving = [zero]
     for g in range(SPAN - 1):
-        arriving.append(ends[g][0:SHARE] + arriving[g] * ends[g][2 * SHARE : 2 * SHARE + 1])
-        into[g + 1, 0:SHARE] = arriving[g + 1]
-        before[g + 1, 0:1] = ends[g][2 * SHARE + 1 : 2 * SHARE + 2]
+        arriving.append(ends[g][0:16] + arriving[g] * spread(ends[g], 2 * DEEP, some, last))
+        into[g + 1] = arriving[g + 1]
+        before[g + 1] = thirds[g]
     returning = zero
-    beyond[SPAN - 1, 0:SHARE] = zero
+    beyond[SPAN - 1] = zero
     for g in range(SPAN - 1, 0, -1):
         returning = (
-            ends[g][SHARE : 2 * SHARE]
-            + arriving[g] * ends[g][2 * SHARE + 1 : 2 * SHARE + 2]
-            + returning * ends[g][2 * SHARE + 2 : 2 * SHARE + 3]
+            ends[g][DEEP : DEEP + 16]
+            + arriving[g] * thirds[g]
+            + returning * spread(ends[g], 2 * DEEP + 2, DEEP + some, last)
         )
-        beyond[g - 1, 0:SHARE] = returning
-    enter = into[mine, 0:SHARE]
+        beyond[g - 1] = returning
+    enter = into[mine]
     front = enter
+    got = [shares[NEAR.index(j)] for j in range(GROUP)]
     fronts = []
     for j in range(GROUP):
-        front = got[j][0:SHARE] + front * got[j][SHARE : SHARE + 1]
+        front = got[j] + front * spread(got[j], DEEP, some, last)
         fronts.append(front)
-    motion = beyond[mine, 0:SHARE]
+    motion = beyond[mine]
     motions = [None] * GROUP
     for j in range(GROUP - 1, -1, -1):
-        motion = fronts[j] + motion * got[j][SHARE + 1 : SHARE + 2]
+        motion = fronts[j] + motion * spread(got[j], DEEP + 1, some + TILES, last)
         motions[j] = motion
-    previous = enter + motion * before[mine, 0:1]
+    previous = enter + motion * before[mine]
+    rest = jnp.zeros((32 - 2 * DEEP, LANES), F32)
     for j in range(GROUP):
-        both = jnp.concatenate([motions[j], previous], axis=0)
-        for t in range(TILES):
-            out[BACK.index(j), 2 * SHARE * t : 2 * SHARE * (t + 1)] = both[:, LANES * t : LANES * (t + 1)]
-        out[BACK.index(j), 2 * SHARE * TILES : 32] = jnp.zeros((32 - 2 * SHARE * TILES, LANES), F32)
+        pieces = [motions[j][0:DEEP], previous[0:DEEP], rest]
+        out[BACK.index(j)] = jnp.concatenate(pieces, axis=0)
         previous = motions[j]
 
 
@@ -149,13 +186,20 @@
 
 
 def stress_body(got, recovery, hotspots, frequency, spectrum, motion_out, out, motion, stern):
+    for part in range(2):
+        rows = slice(HALF * part + HEAD, HALF * (part + 1))
+        motion[rows] = jnp.zeros((PAD, MODES), F32)
+        stern[rows] = jnp.zeros((PAD, MODES), F32)
     for place in range(GROUP):
         d = NEAR.index(BACK[place])
-        for t in range(TILES):
+        t, i = divmod(d, FIVE)
+        pieces = [(t, at, n, skip) for at, n, skip in placed(DEEP * i, DEEP)]
+        if d == LAST:
+            pieces = [(t, HALF + HEAD - TAIL, TAIL, TAIL * t) for t in range(TILES)]
+        for t, at, n, skip in pieces:
             lanes = slice(LANES * t, LANES * (t + 1))
-            rows = slice(SHARE * d, SHARE * (d + 1))
-            motion[rows, lanes] = got[place, 2 * SHARE * t : 2 * SHARE * t + SHARE]
-            stern[rows, lanes] = got[place, 2 * SHARE * t + SHARE : 2 * SHARE * (t + 1)]
+            motion[at : at + n, lanes] = got[place, skip : skip + n]
+            stern[at : at + n, lanes] = got[place, DEEP + skip : DEEP + skip + n]
     motion_out[0, 0, :, 0, :] = motion[0:HEAD]
     motion_out[0, 0, :, 1, :] = motion[HALF : HALF + HEAD]
     contract = (((1,), (1,)), ((), ()))
@@ -164,7 +208,7 @@
     ) + lax.dot_general(
         split(motion[...], 2), recovery[0, :, MODES:], contract, preferred_element_type=F32
     )
-    stress = both[0:ROWS] + both[ROWS:]
+    stress = both[0 : 2 * HALF] + both[2 * HALF :]
     power = stress[0:HALF] ** 2 + stress[HALF:] ** 2
     rows = lax.broadcasted_iota(jnp.int32, (HALF, HEAD), 0)
     columns = lax.broadcasted_iota(jnp.int32, (HALF, HEAD), 1)
@@ -211,7 +255,7 @@
     far = [[GROUP * g + j for g in FAR] for j in range(GROUP)]
     (source,) = call(
         source_body,
-        [(GROUP, 8, MODES)],
+        [(GROUP, 16, LANES)],
         jnp.transpose(wave_loads, (0, 1, 3, 2, 4)),
         pivot_inverse,
         forward[0],
@@ -238,7 +282,7 @@
         hotspots,
         frequency,
         spectrum,
-        scratch=[pltpu.VMEM((SPAN, 8, MODES), F32)] * 3,
+        scratch=[pltpu.VMEM((SPAN, 16, LANES), F32)] * 3,
     )
     solved = exchange(solved, "hull", back)
     motion, energy = call(
@@ -249,7 +293,7 @@
         hotspots,
         frequency,
         spectrum,
-        scratch=[pltpu.VMEM((ROWS, MODES), F32)] * 2,
+        scratch=[pltpu.VMEM((2 * HALF, MODES), F32)] * 2,
     )
     energy = exchange(energy, "freq", [WAVES])
     moments, damage = call(damage_body, [(3, HEAD, 1, POINTS), (HEAD, 1, POINTS)], energy)

time: 61.8 us -> 59.6 us (0.964)
  waiting for transfers between devices: 8.12 us -> 6.03 us
    all_to_all x1, waiting for transfers between devices: 8.12 us -> 6.03 us  [exchange(): lax.all_to_all(values, axis, 0, 0, axis_index_groups=groups, tiled=True)]
where the time goes in v4:
time: 59.6 us; the launch traced here: 59 us
  blocking collectives  35.6 us (60%)
  starting transfers between devices  11.6 us (19%)
  waiting for transfers between devices  6.03 us (10%)
  Pallas kernels  4.43 us (7%)
  between operations  1.34 us (2%)
    all_to_all x3, blocking collectives, exchange(): lax.all_to_all(values, axis, 0, 0, axis_index_groups=groups, tiled=True)  35.6 us
    all_to_all x1, starting transfers between devices, exchange(): lax.all_to_all(values, axis, 0, 0, axis_index_groups=groups, tiled=True)  11.6 us
    all_to_all x1, waiting for transfers between devices, exchange(): lax.all_to_all(values, axis, 0, 0, axis_index_groups=groups, tiled=True)  6.03 us
    pallas_call x5, Pallas kernels, call(): pl.pallas_call(body, out_shape=outs, in_specs=[pl.BlockSpec(memory_space=...  4.43 us
  transfers between devices with their start and end apart: 1, of which 1 were waited for; matrix products, arithmetic and copies ran while one was open for 0% of the time, Pallas kernels for 0%

profile of v4, /device:TPU:1, one launch (start us, length us, event | category | flops | bytes accessed | tf_op | source)
XLA Modules:
  0.0 59.0 jit_solution(11339648662165118905)
XLA Ops:
  0.6 2.1 %shard_map.103 = f32[16,16,128]{2,1,0:T(8,128)} custom-call(bf16[1,1,36,2,384]{4,3,2,1,0:T(2,128)(2,1)} %bitcast.6, bf16[1,1,2,384,384]{4,3,2,1,0:T(8,128)(2,1)} %pivot_hbm.1, bf16[1,384]{1,0:T(2,128)(2,1)} %bitcast.7, bf16[1,384]{1,0:T(2,128)(2,1)} %bitcast.8), custom_call_target="tpu_custom_call" | custom-call | tf_op jit(solution)/shard_map/pallas_call | solution.py:29
  2.7 0.0 copy-start
  2.7 15.5 %all_to_all.20.shares = f32[16,16,128]{2,1,0:T(8,128)S(1)} all-to-all(f32[16,16,128]{2,1,0:T(8,128)} %shard_map.103), channel_id=1, replica_groups={{60,56,52,48,44,40,36,32,28,24,20,16,12,8,4,0},{124,120,116,112,108,104..., dimensions={0} | all-to-all | bytes 262144 | tf_op jit(solution)/shard_map/all_to_all | solution.py:249
  18.2 0.7 %shard_map.104 = f32[8,32,128]{2,1,0:T(8,128)} custom-call(f32[16,16,128]{2,1,0:T(8,128)S(1)} %all_to_all.20.shares), custom_call_target="tpu_custom_call" | custom-call | tf_op jit(solution)/shard_map/pallas_call | solution.py:29
  18.9 11.6 %all-to-all-start.1 = ((f32[8,32,128]{2,1,0:T(8,128)}), f32[8,32,128]{2,1,0:T(8,128)S(1)}, u32[]{:S(2)}, u32[]{:S(2)}) async-start(f32[8,32,128]{2,1,0:T(8,128)} %shard_map.104), calls=%async_computation.1 | async-start | bytes 262144 | tf_op jit(solution)/shard_map/all_to_all | solution.py:249
  30.5 0.0 copy-start.1
  30.5 0.0 copy-start.2
  31.2 6.0 %all-to-all-done.1.reached = f32[8,32,128]{2,1,0:T(8,128)S(1)} async-done(((f32[8,32,128]{2,1,0:T(8,128)}), f32[8,32,128]{2,1,0:T(8,128)S(1)}, u32[]{:S(2)}, u32[]{:S(2)}) %all-to-all-start.1) | async-done | bytes 131104 | tf_op jit(solution)/shard_map/all_to_all | solution.py:249
  37.2 0.0 copy-done
  37.2 0.0 copy-done.1
  37.2 0.0 copy-done.2
  37.2 0.1 shard_map.105
  37.4 11.8 %all_to_all.21.got = f32[16,32,128]{2,1,0:T(8,128)S(1)} all-to-all(f32[16,32,128]{2,1,0:T(8,128)S(1)} %shard_map.105), channel_id=1, replica_groups={{16,20,24,28,32,36,40,44,48,52,56,60,0,4,8,12},{80,84,88,92,96,100,104,..., dimensions={0} | all-to-all | bytes 524288 | tf_op jit(solution)/shard_map/all_to_all | solution.py:249
  49.1 0.8 %shard_map.106 = (f32[1,1,36,2,384]{4,3,2,1,0:T(2,128)}, f32[4,40,256]{2,1,0:T(8,128)S(1)}) custom-call(f32[16,32,128]{2,1,0:T(8,128)S(1)} %all_to_all.21.got, bf16[1,256,768]{2,1,0:T(8,128)(2,1)S(1)} %copy-done, s32[1,256]{1,0:T(1,128)S(1)} %copy-done.1, f32[1]{0:T(128)S(6)} %copy.11.frequency, f32[1,36]{1,0:T(1,128)S(1)} %copy-done.2), custom_call_target="tpu_custom_call" | custom-call | tf_op jit(solution)/shard_map/pallas_call | solution.py:29
  49.9 8.3 %all_to_all.22.got = f32[4,40,256]{2,1,0:T(8,128)S(1)} all-to-all(f32[4,40,256]{2,1,0:T(8,128)S(1)} %get-tuple-element.8), channel_id=1, replica_groups={{3,2,1,0},{7,6,5,4},{11,10,9,8},{15,14,13,12},{19,18,17,16},{23,22,21,2..., dimensions={0} | all-to-all | bytes 327680 | tf_op jit(solution)/shard_map/all_to_all | solution.py:249
  58.2 0.7 %shard_map.107 = (f32[3,36,1,256]{3,2,1,0:T(1,128)}, f32[36,1,256]{2,1,0:T(1,128)}) custom-call(f32[4,40,256]{2,1,0:T(8,128)S(1)} %all_to_all.22.got), custom_call_target="tpu_custom_call" | custom-call | tf_op jit(solution)/shard_map/pallas_call | solution.py:29
Async XLA Ops:
  2.7 34.5 %copy-start = (bf16[1,256,768]{2,1,0:T(8,128)(2,1)S(1)}, bf16[1,256,768]{2,1,0:T(8,128)(2,1)}, u32[]{:S(2)}) copy-start(bf16[1,256,768]{2,1,0:T(8,128)(2,1)} %recovery.3) | copy-start | bytes 1179652
  18.9 18.3 %all-to-all-start.1 = ((f32[8,32,128]{2,1,0:T(8,128)}), f32[8,32,128]{2,1,0:T(8,128)S(1)}, u32[]{:S(2)}, u32[]{:S(2)}) async-start(f32[8,32,128]{2,1,0:T(8,128)} %shard_map.104), calls=%async_computation.1 | async-start | bytes 262144 | tf_op jit(solution)/shard_map/all_to_all | solution.py:249
  30.5 6.7 %copy-start.1 = (s32[1,256]{1,0:T(1,128)S(1)}, s32[1,256]{1,0:T(1,128)}, u32[]{:S(2)}) copy-start(s32[1,256]{1,0:T(1,128)} %hotspots.3) | copy-start | bytes 3076
  30.5 6.7 %copy-start.2 = (f32[1,36]{1,0:T(1,128)S(1)}, f32[1,36]{1,0:T(1,128)}, u32[]{:S(2)}) copy-start(f32[1,36]{1,0:T(1,128)} %spectrum.3) | copy-start | bytes 436

commit v5 on v4

--- a/solution.py
+++ b/solution.py
@@ -17,20 +17,21 @@
 ENDS = 32
 NEAR = (15, 14, 13, 12, 11, 10, 9, 8, 7, 6, 5, 4, 3, 2, 1, 0)
 BACK = (4, 5, 6, 7, 8, 9, 10, 11, 12, 13, 14, 15, 0, 1, 2, 3)
-FAR = (5, 1, 0, 2, 7, 3, 6, 4)
-WAVES = (3, 2, 1, 0)
+FAR = (5, 0, 1, 2, 3, 4, 6, 7)
+WAVES = (2, 3, 1, 0)
 F32 = jnp.float32
 BF16 = jnp.bfloat16
 
 
-def call(body, shapes, *args, spaces=None, vmem_mib=12, scratch=()):
+def call(body, shapes, *args, spaces=None, out_spaces=None, vmem_mib=12, scratch=()):
     outs = [jax.ShapeDtypeStruct(shape, F32) for shape in shapes]
     spaces = spaces or [pltpu.VMEM] * len(args)
+    out_spaces = out_spaces or [pltpu.VMEM] * len(outs)
     return pl.pallas_call(
         body,
         out_shape=outs,
         in_specs=[pl.BlockSpec(memory_space=space) for space in spaces],
-        out_specs=[pl.BlockSpec(memory_space=pltpu.VMEM)] * len(outs),
+        out_specs=[pl.BlockSpec(memory_space=space) for space in out_spaces],
         scratch_shapes=list(scratch),
         compiler_params=pltpu.CompilerParams(vmem_limit_bytes=vmem_mib * 2**20),
     )(*args)
@@ -100,7 +101,7 @@
     return [matrix[TAIL * t : TAIL * t + 1] for t in range(TILES)]
 
 
-def reduce_body(shares, out):
+def reduce_body(shares, recovery, hotspots, frequency, spectrum, out):
     last = is_last()
     got = [shares[NEAR.index(j)] for j in range(GROUP)]
     fores = [spread(block, DEEP, TILES * TAIL, last) for block in got]
@@ -133,7 +134,7 @@
         out[place] = jnp.where(mine < FAR[place], ahead, aft)
 
 
-def solve_body(shares, reached, recovery, hotspots, frequency, spectrum, out, into, beyond, before):
+def solve_body(shares, reached, out, into, beyond, before):
     mine = lax.axis_index("hull") // GROUP
     last = is_last()
     some = TILES * TAIL
@@ -271,17 +272,13 @@
         ],
     )
     shares = exchange(source, "hull", near)
-    (ends,) = call(reduce_body, [(SPAN, ENDS, LANES)], shares)
+    (ends,) = call(reduce_body, [(SPAN, ENDS, LANES)], shares, recovery, hotspots, frequency, spectrum)
     ends = exchange(ends, "hull", far)
     (solved,) = call(
         solve_body,
         [(GROUP, 32, LANES)],
         shares,
         ends,
-        recovery,
-        hotspots,
-        frequency,
-        spectrum,
         scratch=[pltpu.VMEM((SPAN, 16, LANES), F32)] * 3,
     )
     solved = exchange(solved, "hull", back)

time: 59.6 us -> 58.1 us (0.975)
  waiting for transfers between devices: 6.03 us -> 3.05 us
  blocking collectives: 35.6 us -> 37.4 us
    all_to_all x1, waiting for transfers between devices: 6.03 us -> 3.05 us  [exchange(): lax.all_to_all(values, axis, 0, 0, axis_index_groups=groups, tiled=True)]
    all_to_all x3, blocking collectives: 35.6 us -> 37.4 us  [exchange(): lax.all_to_all(values, axis, 0, 0, axis_index_groups=groups, tiled=True)]
where the time goes in v5:
time: 58.1 us; the launch traced here: 57.3 us
  blocking collectives  37.4 us (64%)
  starting transfers between devices  11.6 us (20%)
  Pallas kernels  3.84 us (7%)
  waiting for transfers between devices  3.05 us (5%)
  between operations  1.34 us (2%)
    all_to_all x3, blocking collectives, exchange(): lax.all_to_all(values, axis, 0, 0, axis_index_groups=groups, tiled=True)  37.4 us
    all_to_all x1, starting transfers between devices, exchange(): lax.all_to_all(values, axis, 0, 0, axis_index_groups=groups, tiled=True)  11.6 us
    pallas_call x5, Pallas kernels, call(): pl.pallas_call(body, out_shape=outs, in_specs=[pl.BlockSpec(memory_space=...  3.84 us
    all_to_all x1, waiting for transfers between devices, exchange(): lax.all_to_all(values, axis, 0, 0, axis_index_groups=groups, tiled=True)  3.05 us
  transfers between devices with their start and end apart: 1, of which 1 were waited for; matrix products, arithmetic and copies ran while one was open for 0% of the time, Pallas kernels for 0%

profile of v5, /device:TPU:1, one launch (start us, length us, event | category | flops | bytes accessed | tf_op | source)
XLA Modules:
  0.0 57.3 jit_solution(10491734441135705454)
XLA Ops:
  0.6 0.0 copy-start
  0.6 2.1 %shard_map.103 = f32[16,16,128]{2,1,0:T(8,128)} custom-call(bf16[1,1,36,2,384]{4,3,2,1,0:T(2,128)(2,1)} %bitcast.6, bf16[1,1,2,384,384]{4,3,2,1,0:T(8,128)(2,1)} %pivot_hbm.1, bf16[1,384]{1,0:T(2,128)(2,1)} %bitcast.7, bf16[1,384]{1,0:T(2,128)(2,1)} %bitcast.8), custom_call_target="tpu_custom_call" | custom-call | tf_op jit(solution)/shard_map/pallas_call | solution.py:30
  2.8 11.6 %all-to-all-start = ((f32[16,16,128]{2,1,0:T(8,128)}), f32[16,16,128]{2,1,0:T(8,128)S(1)}, u32[]{:S(2)}, u32[]{:S(2)}) async-start(f32[16,16,128]{2,1,0:T(8,128)} %shard_map.103), calls=%async_computation | async-start | bytes 262144 | tf_op jit(solution)/shard_map/all_to_all | solution.py:250
  14.4 0.0 copy-start.1
  14.4 0.0 copy-start.2
  15.1 3.0 %all-to-all-done.shares = f32[16,16,128]{2,1,0:T(8,128)S(1)} async-done(((f32[16,16,128]{2,1,0:T(8,128)}), f32[16,16,128]{2,1,0:T(8,128)S(1)}, u32[]{:S(2)}, u32[]{:S(2)}) %all-to-all-start) | async-done | bytes 131104 | tf_op jit(solution)/shard_map/all_to_all | solution.py:250
  18.1 0.0 copy-done
  18.1 0.0 copy-done.1
  18.1 0.0 copy-done.2
  18.1 0.1 shard_map.104
  18.2 17.1 %all_to_all.20.reached = f32[8,32,128]{2,1,0:T(8,128)S(1)} all-to-all(f32[8,32,128]{2,1,0:T(8,128)S(1)} %shard_map.104), channel_id=1, replica_groups={{320,0,64,128,192,256,384,448},{324,4,68,132,196,260,388,452},{328,8,72..., dimensions={0} | all-to-all | bytes 262144 | tf_op jit(solution)/shard_map/all_to_all | solution.py:250
  35.3 0.1 shard_map.105
  35.4 12.8 %all_to_all.21.got = f32[16,32,128]{2,1,0:T(8,128)S(1)} all-to-all(f32[16,32,128]{2,1,0:T(8,128)S(1)} %shard_map.105), channel_id=1, replica_groups={{16,20,24,28,32,36,40,44,48,52,56,60,0,4,8,12},{80,84,88,92,96,100,104,..., dimensions={0} | all-to-all | bytes 524288 | tf_op jit(solution)/shard_map/all_to_all | solution.py:250
  48.2 0.8 %shard_map.106 = (f32[1,1,36,2,384]{4,3,2,1,0:T(2,128)}, f32[4,40,256]{2,1,0:T(8,128)S(1)}) custom-call(f32[16,32,128]{2,1,0:T(8,128)S(1)} %all_to_all.21.got, bf16[1,256,768]{2,1,0:T(8,128)(2,1)S(1)} %copy-done, s32[1,256]{1,0:T(1,128)S(1)} %copy-done.1, f32[1]{0:T(128)S(6)} %copy.11.frequency, f32[1,36]{1,0:T(1,128)S(1)} %copy-done.2), custom_call_target="tpu_custom_call" | custom-call | tf_op jit(solution)/shard_map/pallas_call | solution.py:30
  49.0 7.6 %all_to_all.22.got = f32[4,40,256]{2,1,0:T(8,128)S(1)} all-to-all(f32[4,40,256]{2,1,0:T(8,128)S(1)} %get-tuple-element.8), channel_id=1, replica_groups={{2,3,1,0},{6,7,5,4},{10,11,9,8},{14,15,13,12},{18,19,17,16},{22,23,21,2..., dimensions={0} | all-to-all | bytes 327680 | tf_op jit(solution)/shard_map/all_to_all | solution.py:250
  56.6 0.7 %shard_map.107 = (f32[3,36,1,256]{3,2,1,0:T(1,128)}, f32[36,1,256]{2,1,0:T(1,128)}) custom-call(f32[4,40,256]{2,1,0:T(8,128)S(1)} %all_to_all.22.got), custom_call_target="tpu_custom_call" | custom-call | tf_op jit(solution)/shard_map/pallas_call | solution.py:30
Async XLA Ops:
  0.6 17.5 %copy-start = (bf16[1,256,768]{2,1,0:T(8,128)(2,1)S(1)}, bf16[1,256,768]{2,1,0:T(8,128)(2,1)}, u32[]{:S(2)}) copy-start(bf16[1,256,768]{2,1,0:T(8,128)(2,1)} %recovery.3) | copy-start | bytes 1179652
  2.8 15.4 %all-to-all-start = ((f32[16,16,128]{2,1,0:T(8,128)}), f32[16,16,128]{2,1,0:T(8,128)S(1)}, u32[]{:S(2)}, u32[]{:S(2)}) async-start(f32[16,16,128]{2,1,0:T(8,128)} %shard_map.103), calls=%async_computation | async-start | bytes 262144 | tf_op jit(solution)/shard_map/all_to_all | solution.py:250
  14.4 3.7 %copy-start.1 = (s32[1,256]{1,0:T(1,128)S(1)}, s32[1,256]{1,0:T(1,128)}, u32[]{:S(2)}) copy-start(s32[1,256]{1,0:T(1,128)} %hotspots.3) | copy-start | bytes 3076
  14.4 3.7 %copy-start.2 = (f32[1,36]{1,0:T(1,128)S(1)}, f32[1,36]{1,0:T(1,128)}, u32[]{:S(2)}) copy-start(f32[1,36]{1,0:T(1,128)} %spectrum.3) | copy-start | bytes 436

commit v6 on v5

--- a/solution.py
+++ b/solution.py
@@ -23,8 +23,8 @@
 BF16 = jnp.bfloat16
 
 
-def call(body, shapes, *args, spaces=None, out_spaces=None, vmem_mib=12, scratch=()):
-    outs = [jax.ShapeDtypeStruct(shape, F32) for shape in shapes]
+def call(body, shapes, *args, kind=F32, spaces=None, out_spaces=None, vmem_mib=12, scratch=()):
+    outs = [jax.ShapeDtypeStruct(shape, kind) for shape in shapes]
     spaces = spaces or [pltpu.VMEM] * len(args)
     out_spaces = out_spaces or [pltpu.VMEM] * len(outs)
     return pl.pallas_call(
@@ -49,8 +49,8 @@
         pltpu.make_async_copy(pivot_hbm.at[0, 0, 0], pivot.at[0], arrived.at[3]),
         pltpu.make_async_copy(pivot_hbm.at[0, 0, 1], pivot.at[1], arrived.at[4]),
     ]
-    for copy in copies:
-        copy.start()
+    for i in (3, 0, 4, 1, 2):
+        copies[i].start()
     copies[0].wait()
     both = loads[...].astype(F32)
     real = padded(both[:, 0, :])
@@ -101,7 +101,7 @@
     return [matrix[TAIL * t : TAIL * t + 1] for t in range(TILES)]
 
 
-def reduce_body(shares, recovery, hotspots, frequency, spectrum, out):
+def reduce_body(shares, picked, frequency, spectrum, out):
     last = is_last()
     got = [shares[NEAR.index(j)] for j in range(GROUP)]
     fores = [spread(block, DEEP, TILES * TAIL, last) for block in got]
@@ -170,10 +170,10 @@
         motion = fronts[j] + motion * spread(got[j], DEEP + 1, some + TILES, last)
         motions[j] = motion
     previous = enter + motion * before[mine]
-    rest = jnp.zeros((32 - 2 * DEEP, LANES), F32)
     for j in range(GROUP):
-        pieces = [motions[j][0:DEEP], previous[0:DEEP], rest]
-        out[BACK.index(j)] = jnp.concatenate(pieces, axis=0)
+        both = jnp.concatenate([motions[j][0:DEEP], previous[0:DEEP]], axis=0)
+        for q in range(2 * DEEP // 4):
+            out[BACK.index(j), q] = both[4 * q : 4 * q + 4]
         previous = motions[j]
 
 
@@ -186,28 +186,37 @@
     return jnp.concatenate(pieces, axis=0)
 
 
-def stress_body(got, recovery, hotspots, frequency, spectrum, motion_out, out, motion, stern):
+def pick_body(recovery, hotspots, picked):
+    elements = lax.broadcasted_iota(jnp.int32, (POINTS, POINTS), 0)
+    chosen = jnp.where(elements == hotspots[...], 1.0, 0.0).astype(BF16)
+    contract = (((0,), (0,)), ((), ()))
+    rows = lax.dot_general(chosen, recovery[0], contract, preferred_element_type=F32)
+    picked[...] = rows.astype(BF16)
+
+
+def stress_body(got, picked, frequency, spectrum, motion_out, out, motion, stern):
     for part in range(2):
         rows = slice(HALF * part + HEAD, HALF * (part + 1))
         motion[rows] = jnp.zeros((PAD, MODES), F32)
         stern[rows] = jnp.zeros((PAD, MODES), F32)
     for place in range(GROUP):
         d = NEAR.index(BACK[place])
+        block = jnp.concatenate([got[place, q] for q in range(2 * DEEP // 4)], axis=0)
         t, i = divmod(d, FIVE)
         pieces = [(t, at, n, skip) for at, n, skip in placed(DEEP * i, DEEP)]
         if d == LAST:
             pieces = [(t, HALF + HEAD - TAIL, TAIL, TAIL * t) for t in range(TILES)]
         for t, at, n, skip in pieces:
             lanes = slice(LANES * t, LANES * (t + 1))
-            motion[at : at + n, lanes] = got[place, skip : skip + n]
-            stern[at : at + n, lanes] = got[place, DEEP + skip : DEEP + skip + n]
+            motion[at : at + n, lanes] = block[skip : skip + n]
+            stern[at : at + n, lanes] = block[DEEP + skip : DEEP + skip + n]
     motion_out[0, 0, :, 0, :] = motion[0:HEAD]
     motion_out[0, 0, :, 1, :] = motion[HALF : HALF + HEAD]
     contract = (((1,), (1,)), ((), ()))
     both = lax.dot_general(
-        split(stern[...], 2), recovery[0, :, 0:MODES], contract, preferred_element_type=F32
+        split(stern[...], 2), picked[:, 0:MODES], contract, preferred_element_type=F32
     ) + lax.dot_general(
-        split(motion[...], 2), recovery[0, :, MODES:], contract, preferred_element_type=F32
+        split(motion[...], 2), picked[:, MODES:], contract, preferred_element_type=F32
     )
     stress = both[0 : 2 * HALF] + both[2 * HALF :]
     power = stress[0:HALF] ** 2 + stress[HALF:] ** 2
@@ -215,10 +224,6 @@
     columns = lax.broadcasted_iota(jnp.int32, (HALF, HEAD), 1)
     weight = jnp.sum(jnp.where(rows == columns, spectrum[...], 0.0), axis=1, keepdims=True)
     energy = power * (weight * (1.2 / 4))
-    elements = lax.broadcasted_iota(jnp.int32, (POINTS, POINTS), 0)
-    chosen = jnp.where(elements == hotspots[...], 1.0, 0.0).astype(BF16)
-    thirds = jnp.dot(split(energy, 3), chosen, preferred_element_type=F32)
-    energy = thirds[0:HALF] + (thirds[HALF : 2 * HALF] + thirds[2 * HALF :])
     here = jnp.broadcast_to(frequency[...].reshape(1, 1), (1, POINTS))
     rows = lax.broadcasted_iota(jnp.int32, (HALF, POINTS), 0)
     packed = jnp.where(rows < HEAD, energy, here)
@@ -271,12 +276,13 @@
             pltpu.SemaphoreType.DMA((5,)),
         ],
     )
+    (picked,) = call(pick_body, [(POINTS, 2 * MODES)], recovery, hotspots, kind=BF16)
     shares = exchange(source, "hull", near)
-    (ends,) = call(reduce_body, [(SPAN, ENDS, LANES)], shares, recovery, hotspots, frequency, spectrum)
+    (ends,) = call(reduce_body, [(SPAN, ENDS, LANES)], shares, picked, frequency, spectrum)
     ends = exchange(ends, "hull", far)
     (solved,) = call(
         solve_body,
-        [(GROUP, 32, LANES)],
+        [(GROUP, 2 * DEEP // 4, 4, LANES)],
         shares,
         ends,
         scratch=[pltpu.VMEM((SPAN, 16, LANES), F32)] * 3,
@@ -286,8 +292,7 @@
         stress_body,
         [(1, 1, HEAD, 2, MODES), (4, HALF, POINTS)],
         solved,
-        recovery,
-        hotspots,
+        picked,
         frequency,
         spectrum,
         scratch=[pltpu.VMEM((2 * HALF, MODES), F32)] * 2,

time: 58.1 us -> 57.7 us (level)
    pallas_call x5 -> x6, Pallas kernels: 3.84 us -> 4.07 us  [call(): pl.pallas_call(body, out_shape=outs, in_specs=[pl.BlockSpec(memory_space=...]
  transfers between devices with their start and end apart: 1 -> 1, of which waited for: 1 -> 1; matrix products, arithmetic and copies ran while one was open for 0% -> 0% of each run, Pallas kernels for 0% -> 1%
where the time goes in v6:
time: 57.7 us; the launch traced here: 57 us
  blocking collectives  37.2 us (64%)
  starting transfers between devices  11.6 us (20%)
  Pallas kernels  4.07 us (7%)
  waiting for transfers between devices  2.72 us (5%)
  between operations  1.36 us (2%)
    all_to_all x3, blocking collectives, exchange(): lax.all_to_all(values, axis, 0, 0, axis_index_groups=groups, tiled=True)  37.2 us
    all_to_all x1, starting transfers between devices, exchange(): lax.all_to_all(values, axis, 0, 0, axis_index_groups=groups, tiled=True)  11.6 us
    pallas_call x6, Pallas kernels, call(): pl.pallas_call(body, out_shape=outs, in_specs=[pl.BlockSpec(memory_space=...  4.07 us
    all_to_all x1, waiting for transfers between devices, exchange(): lax.all_to_all(values, axis, 0, 0, axis_index_groups=groups, tiled=True)  2.72 us
  transfers between devices with their start and end apart: 1, of which 1 were waited for; matrix products, arithmetic and copies ran while one was open for 0% of the time, Pallas kernels for 1%

profile of v6, /device:TPU:1, one launch (start us, length us, event | category | flops | bytes accessed | tf_op | source)
XLA Modules:
  0.0 57.0 jit_solution(11933111830932310831)
XLA Ops:
  0.6 0.0 copy-start
  0.6 2.1 %shard_map.103 = f32[16,16,128]{2,1,0:T(8,128)} custom-call(bf16[1,1,36,2,384]{4,3,2,1,0:T(2,128)(2,1)} %bitcast.6, bf16[1,1,2,384,384]{4,3,2,1,0:T(8,128)(2,1)} %pivot_hbm.1, bf16[1,384]{1,0:T(2,128)(2,1)} %bitcast.7, bf16[1,384]{1,0:T(2,128)(2,1)} %bitcast.8), custom_call_target="tpu_custom_call" | custom-call | tf_op jit(solution)/shard_map/pallas_call | solution.py:30
  2.7 11.6 %all-to-all-start = ((f32[16,16,128]{2,1,0:T(8,128)}), f32[16,16,128]{2,1,0:T(8,128)S(1)}, u32[]{:S(2)}, u32[]{:S(2)}) async-start(f32[16,16,128]{2,1,0:T(8,128)} %shard_map.103), calls=%async_computation | async-start | bytes 262144 | tf_op jit(solution)/shard_map/all_to_all | solution.py:255
  14.4 0.0 copy-start.2
  15.0 0.0 copy-done
  15.0 0.0 copy-done.2
  15.0 0.0 copy-start.1
  15.1 0.3 shard_map.104.picked
  15.4 2.7 %all-to-all-done.shares = f32[16,16,128]{2,1,0:T(8,128)S(1)} async-done(((f32[16,16,128]{2,1,0:T(8,128)}), f32[16,16,128]{2,1,0:T(8,128)S(1)}, u32[]{:S(2)}, u32[]{:S(2)}) %all-to-all-start) | async-done | bytes 131104 | tf_op jit(solution)/shard_map/all_to_all | solution.py:255
  18.1 0.0 copy-done.1
  18.1 0.1 shard_map.105
  18.2 17.1 %all_to_all.20.reached = f32[8,32,128]{2,1,0:T(8,128)S(1)} all-to-all(f32[8,32,128]{2,1,0:T(8,128)S(1)} %shard_map.105), channel_id=1, replica_groups={{320,0,64,128,192,256,384,448},{324,4,68,132,196,260,388,452},{328,8,72..., dimensions={0} | all-to-all | bytes 262144 | tf_op jit(solution)/shard_map/all_to_all | solution.py:255
  35.2 0.1 shard_map.106
  35.4 12.6 %all_to_all.21.got = f32[16,7,4,128]{3,2,1,0:T(4,128)S(1)} all-to-all(f32[16,7,4,128]{3,2,1,0:T(4,128)S(1)} %shard_map.106), channel_id=1, replica_groups={{16,20,24,28,32,36,40,44,48,52,56,60,0,4,8,12},{80,84,88,92,96,100,104,..., dimensions={0} | all-to-all | bytes 458752 | tf_op jit(solution)/shard_map/all_to_all | solution.py:255
  47.9 0.8 %shard_map.107 = (f32[1,1,36,2,384]{4,3,2,1,0:T(2,128)}, f32[4,40,256]{2,1,0:T(8,128)S(1)}) custom-call(f32[16,7,4,128]{3,2,1,0:T(4,128)S(1)} %all_to_all.21.got, bf16[256,768]{1,0:T(8,128)(2,1)S(1)} %shard_map.104.picked, f32[1]{0:T(128)S(6)} %copy.11.frequency, f32[1,36]{1,0:T(1,128)S(1)} %copy-done.1), custom_call_target="tpu_custom_call" | custom-call | tf_op jit(solution)/shard_map/pallas_call | solution.py:30
  48.7 7.6 %all_to_all.22.got = f32[4,40,256]{2,1,0:T(8,128)S(1)} all-to-all(f32[4,40,256]{2,1,0:T(8,128)S(1)} %get-tuple-element.8), channel_id=1, replica_groups={{2,3,1,0},{6,7,5,4},{10,11,9,8},{14,15,13,12},{18,19,17,16},{22,23,21,2..., dimensions={0} | all-to-all | bytes 327680 | tf_op jit(solution)/shard_map/all_to_all | solution.py:255
  56.3 0.7 %shard_map.108 = (f32[3,36,1,256]{3,2,1,0:T(1,128)}, f32[36,1,256]{2,1,0:T(1,128)}) custom-call(f32[4,40,256]{2,1,0:T(8,128)S(1)} %all_to_all.22.got), custom_call_target="tpu_custom_call" | custom-call | tf_op jit(solution)/shard_map/pallas_call | solution.py:30
Async XLA Ops:
  0.6 14.4 %copy-start = (bf16[1,256,768]{2,1,0:T(8,128)(2,1)S(1)}, bf16[1,256,768]{2,1,0:T(8,128)(2,1)}, u32[]{:S(2)}) copy-start(bf16[1,256,768]{2,1,0:T(8,128)(2,1)} %recovery.1) | copy-start | bytes 1179652
  2.7 15.4 %all-to-all-start = ((f32[16,16,128]{2,1,0:T(8,128)}), f32[16,16,128]{2,1,0:T(8,128)S(1)}, u32[]{:S(2)}, u32[]{:S(2)}) async-start(f32[16,16,128]{2,1,0:T(8,128)} %shard_map.103), calls=%async_computation | async-start | bytes 262144 | tf_op jit(solution)/shard_map/all_to_all | solution.py:255
  14.4 0.7 %copy-start.2 = (s32[1,256]{1,0:T(1,128)S(1)}, s32[1,256]{1,0:T(1,128)}, u32[]{:S(2)}) copy-start(s32[1,256]{1,0:T(1,128)} %hotspots.1) | copy-start | bytes 3076
  15.0 3.0 %copy-start.1 = (f32[1,36]{1,0:T(1,128)S(1)}, f32[1,36]{1,0:T(1,128)}, u32[]{:S(2)}) copy-start(f32[1,36]{1,0:T(1,128)} %spectrum.3) | copy-start | bytes 436

commit v7 on v6

--- a/solution.py
+++ b/solution.py
@@ -231,7 +231,13 @@
         out[f] = packed
 
 
-def damage_body(got, moments_out, damage_out):
+def damage_body(got, motion, moments_out, damage_out, motion_out, moments, damage, sent):
+    copies = [
+        pltpu.make_async_copy(motion, motion_out, sent.at[0]),
+        pltpu.make_async_copy(moments, moments_out, sent.at[1]),
+        pltpu.make_async_copy(damage, damage_out, sent.at[2]),
+    ]
+    copies[0].start()
     zeroth = jnp.zeros((HEAD, POINTS), F32)
     second = zeroth
     fourth = zeroth
@@ -241,14 +247,18 @@
         zeroth = zeroth + energy
         second = second + energy * square
         fourth = fourth + energy * (square * square)
-    moments_out[0, :, 0, :] = zeroth
-    moments_out[1, :, 0, :] = second
-    moments_out[2, :, 0, :] = fourth
-    damage_out[:, 0, :] = (
+    moments[0, :, 0, :] = zeroth
+    moments[1, :, 0, :] = second
+    moments[2, :, 0, :] = fourth
+    copies[1].start()
+    damage[:, 0, :] = (
         0.5 * jnp.log(fourth / second)
         + 1.5 * jnp.log(zeroth)
         + jnp.log(0.5 + 0.5 * second / jnp.sqrt(zeroth * fourth))
     )
+    copies[2].start()
+    for copy in copies:
+        copy.wait()
 
 
 def exchange(values, axis, groups):
@@ -298,7 +308,15 @@
         scratch=[pltpu.VMEM((2 * HALF, MODES), F32)] * 2,
     )
     energy = exchange(energy, "freq", [WAVES])
-    moments, damage = call(damage_body, [(3, HEAD, 1, POINTS), (HEAD, 1, POINTS)], energy)
+    shapes = [(3, HEAD, 1, POINTS), (HEAD, 1, POINTS)]
+    moments, damage, motion = call(
+        damage_body,
+        shapes + [motion.shape],
+        energy,
+        motion,
+        out_spaces=[pltpu.HBM] * 3,
+        scratch=[pltpu.VMEM(shape, F32) for shape in shapes] + [pltpu.SemaphoreType.DMA((3,))],
+    )
     return (
         jnp.transpose(motion, (0, 1, 3, 2, 4)),
         jnp.transpose(moments, (0, 2, 1, 3)),

time: 57.7 us -> 57.3 us (level)
  no operation moved by 1% of the time
where the time goes in v7:
time: 57.3 us; the launch traced here: 56.6 us
  blocking collectives  37.2 us (65%)
  starting transfers between devices  11.6 us (20%)
  Pallas kernels  3.62 us (6%)
  waiting for transfers between devices  2.72 us (5%)
  between operations  1.36 us (2%)
    all_to_all x3, blocking collectives, exchange(): lax.all_to_all(values, axis, 0, 0, axis_index_groups=groups, tiled=True)  37.2 us
    all_to_all x1, starting transfers between devices, exchange(): lax.all_to_all(values, axis, 0, 0, axis_index_groups=groups, tiled=True)  11.6 us
    pallas_call x6, Pallas kernels, call(): pl.pallas_call(body, out_shape=outs, in_specs=[pl.BlockSpec(memory_space=...  3.62 us
    all_to_all x1, waiting for transfers between devices, exchange(): lax.all_to_all(values, axis, 0, 0, axis_index_groups=groups, tiled=True)  2.72 us
  transfers between devices with their start and end apart: 1, of which 1 were waited for; matrix products, arithmetic and copies ran while one was open for 0% of the time, Pallas kernels for 1%

profile of v7, /device:TPU:1, one launch (start us, length us, event | category | flops | bytes accessed | tf_op | source)
XLA Modules:
  0.0 56.6 jit_solution(957770764517799668)
XLA Ops:
  0.6 0.0 copy-start
  0.6 2.1 %shard_map.103 = f32[16,16,128]{2,1,0:T(8,128)} custom-call(bf16[1,1,36,2,384]{4,3,2,1,0:T(2,128)(2,1)} %bitcast.6, bf16[1,1,2,384,384]{4,3,2,1,0:T(8,128)(2,1)} %pivot_hbm.1, bf16[1,384]{1,0:T(2,128)(2,1)} %bitcast.7, bf16[1,384]{1,0:T(2,128)(2,1)} %bitcast.8), custom_call_target="tpu_custom_call" | custom-call | tf_op jit(solution)/shard_map/pallas_call | solution.py:30
  2.7 11.6 %all-to-all-start = ((f32[16,16,128]{2,1,0:T(8,128)}), f32[16,16,128]{2,1,0:T(8,128)S(1)}, u32[]{:S(2)}, u32[]{:S(2)}) async-start(f32[16,16,128]{2,1,0:T(8,128)} %shard_map.103), calls=%async_computation | async-start | bytes 262144 | tf_op jit(solution)/shard_map/all_to_all | solution.py:265
  14.4 0.0 copy-start.2
  15.0 0.0 copy-done
  15.0 0.0 copy-done.2
  15.0 0.0 copy-start.1
  15.1 0.3 shard_map.104.picked
  15.4 2.7 %all-to-all-done.shares = f32[16,16,128]{2,1,0:T(8,128)S(1)} async-done(((f32[16,16,128]{2,1,0:T(8,128)}), f32[16,16,128]{2,1,0:T(8,128)S(1)}, u32[]{:S(2)}, u32[]{:S(2)}) %all-to-all-start) | async-done | bytes 131104 | tf_op jit(solution)/shard_map/all_to_all | solution.py:265
  18.1 0.0 copy-done.1
  18.1 0.1 shard_map.105
  18.2 17.1 %all_to_all.20.reached = f32[8,32,128]{2,1,0:T(8,128)S(1)} all-to-all(f32[8,32,128]{2,1,0:T(8,128)S(1)} %shard_map.105), channel_id=1, replica_groups={{320,0,64,128,192,256,384,448},{324,4,68,132,196,260,388,452},{328,8,72..., dimensions={0} | all-to-all | bytes 262144 | tf_op jit(solution)/shard_map/all_to_all | solution.py:265
  35.2 0.1 shard_map.106
  35.4 12.6 %all_to_all.21.got = f32[16,7,4,128]{3,2,1,0:T(4,128)S(1)} all-to-all(f32[16,7,4,128]{3,2,1,0:T(4,128)S(1)} %shard_map.106), channel_id=1, replica_groups={{16,20,24,28,32,36,40,44,48,52,56,60,0,4,8,12},{80,84,88,92,96,100,104,..., dimensions={0} | all-to-all | bytes 458752 | tf_op jit(solution)/shard_map/all_to_all | solution.py:265
  47.9 0.3 shard_map.107
  48.2 7.6 %all_to_all.22.got = f32[4,40,256]{2,1,0:T(8,128)S(1)} all-to-all(f32[4,40,256]{2,1,0:T(8,128)S(1)} %get-tuple-element.8), channel_id=1, replica_groups={{2,3,1,0},{6,7,5,4},{10,11,9,8},{14,15,13,12},{18,19,17,16},{22,23,21,2..., dimensions={0} | all-to-all | bytes 327680 | tf_op jit(solution)/shard_map/all_to_all | solution.py:265
  55.8 0.8 %shard_map.108 = (f32[3,36,1,256]{3,2,1,0:T(1,128)}, f32[36,1,256]{2,1,0:T(1,128)}, f32[1,1,36,2,384]{4,3,2,1,0:T(2,128)}) custom-call(f32[4,40,256]{2,1,0:T(8,128)S(1)} %all_to_all.22.got, f32[1,1,36,2,384]{4,3,2,1,0:T(2,128)S(1)} %get-tuple-element.9.motion), custom_call_target="tpu_custom_call" | custom-call | tf_op jit(solution)/shard_map/pallas_call | solution.py:30
Async XLA Ops:
  0.6 14.4 %copy-start = (bf16[1,256,768]{2,1,0:T(8,128)(2,1)S(1)}, bf16[1,256,768]{2,1,0:T(8,128)(2,1)}, u32[]{:S(2)}) copy-start(bf16[1,256,768]{2,1,0:T(8,128)(2,1)} %recovery.1) | copy-start | bytes 1179652
  2.7 15.4 %all-to-all-start = ((f32[16,16,128]{2,1,0:T(8,128)}), f32[16,16,128]{2,1,0:T(8,128)S(1)}, u32[]{:S(2)}, u32[]{:S(2)}) async-start(f32[16,16,128]{2,1,0:T(8,128)} %shard_map.103), calls=%async_computation | async-start | bytes 262144 | tf_op jit(solution)/shard_map/all_to_all | solution.py:265
  14.4 0.7 %copy-start.2 = (s32[1,256]{1,0:T(1,128)S(1)}, s32[1,256]{1,0:T(1,128)}, u32[]{:S(2)}) copy-start(s32[1,256]{1,0:T(1,128)} %hotspots.1) | copy-start | bytes 3076
  15.0 3.0 %copy-start.1 = (f32[1,36]{1,0:T(1,128)S(1)}, f32[1,36]{1,0:T(1,128)}, u32[]{:S(2)}) copy-start(f32[1,36]{1,0:T(1,128)} %spectrum.3) | copy-start | bytes 436

commit v8 on v7

--- a/solution.py
+++ b/solution.py
@@ -16,9 +16,9 @@
 LAST = FIVE * TILES
 ENDS = 32
 NEAR = (15, 14, 13, 12, 11, 10, 9, 8, 7, 6, 5, 4, 3, 2, 1, 0)
-BACK = (4, 5, 6, 7, 8, 9, 10, 11, 12, 13, 14, 15, 0, 1, 2, 3)
+BACK = (15, 14, 13, 12, 11, 10, 9, 8, 7, 6, 5, 4, 3, 2, 1, 0)
 FAR = (5, 0, 1, 2, 3, 4, 6, 7)
-WAVES = (2, 3, 1, 0)
+WAVES = (2, 0, 1, 3)
 F32 = jnp.float32
 BF16 = jnp.bfloat16
 

time: 57.3 us -> 57.4 us (level)
  no operation moved by 1% of the time
where the time goes in v8:
time: 57.4 us; the launch traced here: 57.1 us
  blocking collectives  37.7 us (66%)
  starting transfers between devices  11.6 us (20%)
  Pallas kernels  3.63 us (6%)
  waiting for transfers between devices  2.72 us (5%)
  between operations  1.36 us (2%)
    all_to_all x3, blocking collectives, exchange(): lax.all_to_all(values, axis, 0, 0, axis_index_groups=groups, tiled=True)  37.7 us
    all_to_all x1, starting transfers between devices, exchange(): lax.all_to_all(values, axis, 0, 0, axis_index_groups=groups, tiled=True)  11.6 us
    pallas_call x6, Pallas kernels, call(): pl.pallas_call(body, out_shape=outs, in_specs=[pl.BlockSpec(memory_space=...  3.63 us
    all_to_all x1, waiting for transfers between devices, exchange(): lax.all_to_all(values, axis, 0, 0, axis_index_groups=groups, tiled=True)  2.72 us
  transfers between devices with their start and end apart: 1, of which 1 were waited for; matrix products, arithmetic and copies ran while one was open for 0% of the time, Pallas kernels for 1%

profile of v8, /device:TPU:1, one launch (start us, length us, event | category | flops | bytes accessed | tf_op | source)
XLA Modules:
  0.0 57.1 jit_solution(2060469047529844911)
XLA Ops:
  0.6 0.0 copy-start
  0.6 2.1 %shard_map.103 = f32[16,16,128]{2,1,0:T(8,128)} custom-call(bf16[1,1,36,2,384]{4,3,2,1,0:T(2,128)(2,1)} %bitcast.6, bf16[1,1,2,384,384]{4,3,2,1,0:T(8,128)(2,1)} %pivot_hbm.1, bf16[1,384]{1,0:T(2,128)(2,1)} %bitcast.7, bf16[1,384]{1,0:T(2,128)(2,1)} %bitcast.8), custom_call_target="tpu_custom_call" | custom-call | tf_op jit(solution)/shard_map/pallas_call | solution.py:30
  2.7 11.6 %all-to-all-start = ((f32[16,16,128]{2,1,0:T(8,128)}), f32[16,16,128]{2,1,0:T(8,128)S(1)}, u32[]{:S(2)}, u32[]{:S(2)}) async-start(f32[16,16,128]{2,1,0:T(8,128)} %shard_map.103), calls=%async_computation | async-start | bytes 262144 | tf_op jit(solution)/shard_map/all_to_all | solution.py:265
  14.4 0.0 copy-start.2
  15.0 0.0 copy-done
  15.0 0.0 copy-done.2
  15.0 0.0 copy-start.1
  15.1 0.3 shard_map.104.picked
  15.4 2.7 %all-to-all-done.shares = f32[16,16,128]{2,1,0:T(8,128)S(1)} async-done(((f32[16,16,128]{2,1,0:T(8,128)}), f32[16,16,128]{2,1,0:T(8,128)S(1)}, u32[]{:S(2)}, u32[]{:S(2)}) %all-to-all-start) | async-done | bytes 131104 | tf_op jit(solution)/shard_map/all_to_all | solution.py:265
  18.1 0.0 copy-done.1
  18.1 0.1 shard_map.105
  18.2 17.1 %all_to_all.20.reached = f32[8,32,128]{2,1,0:T(8,128)S(1)} all-to-all(f32[8,32,128]{2,1,0:T(8,128)S(1)} %shard_map.105), channel_id=1, replica_groups={{320,0,64,128,192,256,384,448},{324,4,68,132,196,260,388,452},{328,8,72..., dimensions={0} | all-to-all | bytes 262144 | tf_op jit(solution)/shard_map/all_to_all | solution.py:265
  35.2 0.1 shard_map.106
  35.4 12.5 %all_to_all.21.got = f32[16,7,4,128]{3,2,1,0:T(4,128)S(1)} all-to-all(f32[16,7,4,128]{3,2,1,0:T(4,128)S(1)} %shard_map.106), channel_id=1, replica_groups={{60,56,52,48,44,40,36,32,28,24,20,16,12,8,4,0},{124,120,116,112,108,104..., dimensions={0} | all-to-all | bytes 458752 | tf_op jit(solution)/shard_map/all_to_all | solution.py:265
  47.9 0.3 shard_map.107
  48.2 8.1 %all_to_all.22.got = f32[4,40,256]{2,1,0:T(8,128)S(1)} all-to-all(f32[4,40,256]{2,1,0:T(8,128)S(1)} %get-tuple-element.8), channel_id=1, replica_groups={{2,0,1,3},{6,4,5,7},{10,8,9,11},{14,12,13,15},{18,16,17,19},{22,20,21,2..., dimensions={0} | all-to-all | bytes 327680 | tf_op jit(solution)/shard_map/all_to_all | solution.py:265
  56.3 0.8 %shard_map.108 = (f32[3,36,1,256]{3,2,1,0:T(1,128)}, f32[36,1,256]{2,1,0:T(1,128)}, f32[1,1,36,2,384]{4,3,2,1,0:T(2,128)}) custom-call(f32[4,40,256]{2,1,0:T(8,128)S(1)} %all_to_all.22.got, f32[1,1,36,2,384]{4,3,2,1,0:T(2,128)S(1)} %get-tuple-element.9.motion), custom_call_target="tpu_custom_call" | custom-call | tf_op jit(solution)/shard_map/pallas_call | solution.py:30
Async XLA Ops:
  0.6 14.4 %copy-start = (bf16[1,256,768]{2,1,0:T(8,128)(2,1)S(1)}, bf16[1,256,768]{2,1,0:T(8,128)(2,1)}, u32[]{:S(2)}) copy-start(bf16[1,256,768]{2,1,0:T(8,128)(2,1)} %recovery.1) | copy-start | bytes 1179652
  2.7 15.4 %all-to-all-start = ((f32[16,16,128]{2,1,0:T(8,128)}), f32[16,16,128]{2,1,0:T(8,128)S(1)}, u32[]{:S(2)}, u32[]{:S(2)}) async-start(f32[16,16,128]{2,1,0:T(8,128)} %shard_map.103), calls=%async_computation | async-start | bytes 262144 | tf_op jit(solution)/shard_map/all_to_all | solution.py:265
  14.4 0.7 %copy-start.2 = (s32[1,256]{1,0:T(1,128)S(1)}, s32[1,256]{1,0:T(1,128)}, u32[]{:S(2)}) copy-start(s32[1,256]{1,0:T(1,128)} %hotspots.1) | copy-start | bytes 3076
  15.0 3.0 %copy-start.1 = (f32[1,36]{1,0:T(1,128)S(1)}, f32[1,36]{1,0:T(1,128)}, u32[]{:S(2)}) copy-start(f32[1,36]{1,0:T(1,128)} %spectrum.3) | copy-start | bytes 436
